TPU v7x, 32 devices: a whole 2x2x4 slice. The times are simulated.
32 devices in a mesh: member: 2 (over y), comp: 4 (over z), lev: 2 (over x), sub: 2 (over core).
Axes of the slice: x: 2, y: 2, z: 4, core: 2. Of those that a mesh axis runs over, the one named last changes fastest.
Arguments:
- atmos_state: float32 [4, 72, 8192], P(None, 'lev', ('member', 'comp', 'sub')), parts along dimension 2, may hold values from -6 to 6
- ocean_state: float32 [2, 80, 8192], P(None, None, ('member', 'comp', 'lev', 'sub')), parts along dimension 2, may hold values from -6 to 6
- level_weight: float32 [72], P('lev'), may hold values from 0.02 to 0.2
- atmos_neighbors: int32 [4, 4096], P(None, ('comp', 'sub')), may hold values from 0 to 639, as said below
- atmos_diffusion: float32 [4, 4096], P(None, ('comp', 'sub')), may hold values from 0.05 to 0.24
- ocean_neighbors: int32 [6, 4096], P(None, ('comp', 'lev', 'sub')), may hold values from 0 to 383, as said below
- ocean_diffusion: float32 [6, 4096], P(None, ('comp', 'lev', 'sub')), may hold values from 0.03 to 0.16
- vertical_mixing: float32 [4096], P(('comp', 'lev', 'sub')), may hold values from 0.05 to 0.45
- send_columns: int32 [4096], P(('comp', 'lev', 'sub')), may hold values from 0 to 511
- read_slots: int32 [4, 4096], P(None, ('comp', 'lev', 'sub')), may hold values from 0 to 255, as said below
- remap_weight: float32 [4, 4096], P(None, ('comp', 'lev', 'sub')), may hold values from 0.1 to 1
Outputs:
- atmos_out: float32 [4, 72, 8192], P(None, 'lev', ('member', 'comp', 'sub')), parts along dimension 2
- ocean_out: float32 [2, 80, 8192], P(None, None, ('member', 'comp', 'lev', 'sub')), parts along dimension 2
There are 2 independent parts, one for each index of `member`. A program takes and returns all parts, laid end to end along the dimension named above; an argument that names none is the same for every part. Nothing has to cross between parts.
Inputs may be any that keep to these rules, and one draw needn't show every extreme that they name: `atmos_neighbors`: entry n of a column or cell in block b names place e of the block extended by 64 on each side: the neighbour is element 512 b + e - 64 of the whole, taken around the end. Every neighbour lies within 64 of the column. `ocean_neighbors`: as for the atmosphere, with blocks of 256 cells. `send_columns`: places 8 and up that a device fills for a position of its lev group are read only where that position is its own or adjacent to it, modulo 8. `read_slots`: A cell of a device at position d reads source position p = slot // 32 at place slot % 32; places of 8 and up only where p is d - 1, d or d + 1 modulo 8. Every place that may be read is read by some cell of the device.
All inputs are finite; a program needn't handle non-finite values.
Results may differ from a plain program's by a relative error of at most 0.0003.
Values sent between devices are 32-bit elements; how exact they have to be, the bound alone decides.
A program may use at most 64 MiB of HBM per device.

v0:
```python
import jax
import jax.numpy as jnp
from jax import lax
from jax.sharding import PartitionSpec as P

HALO = 64
STEPS_ATM = 4
STEPS_OCN = 2


def padded_2(value, sides, width):
    for axis, dim in sides:
        count, length = (lax.axis_size(axis), value.shape[dim])
        up = [(i, (i + 1) % count) for i in range(count)]
        down = [(j, i) for i, j in up]
        last = lax.slice_in_dim(value, length - width, length, axis=dim)
        initial = lax.slice_in_dim(value, 0, width, axis=dim)
        before = lax.ppermute(last, axis, up)
        after = lax.ppermute(initial, axis, down)
        value = jnp.concatenate([before, value, after], axis=dim)
    return value


def mixing_matrix(places, rates, span, offset):
    columns = places.shape[1]
    row_ids = jnp.arange(span, dtype=jnp.int32)[:, None]
    column_ids = jnp.arange(columns, dtype=jnp.int32)[None, :]
    matrix = jnp.zeros((span, columns), jnp.float32)
    for column_slot in range(places.shape[0]):
        matrix = matrix + jnp.where(
            row_ids == places[column_slot][None, :], rates[column_slot][None, :], 0.0
        )
    keep = 1.0 - jnp.sum(rates, axis=0)
    matrix = matrix + jnp.where(row_ids == column_ids + offset, keep[None, :], 0.0)
    return matrix


def apply_mix(padded, matrix):
    leading = padded.shape[:-1]
    flat = padded.reshape(-1, padded.shape[-1])
    result = jnp.dot(
        flat, matrix, precision=lax.Precision.HIGHEST, preferred_element_type=jnp.float32
    )
    return result.reshape(leading + (matrix.shape[1],))


def vertical(sea_state, mixing):
    upper_level = jnp.concatenate([sea_state[:, :1], sea_state[:, :-1]], axis=1)
    lower_level = jnp.concatenate([sea_state[:, 1:], sea_state[:, -1:]], axis=1)
    return sea_state + mixing * (upper_level - 2.0 * sea_state + lower_level)


def force(sea_state, remapped):
    surface_temp = sea_state[0, 0]
    surface_salt = sea_state[1, 0]
    wind_speed = jnp.sqrt(remapped[2] * remapped[2] + remapped[3] * remapped[3] + 1.0)
    evaporation = 0.2 * wind_speed * (0.5 * jnp.exp(0.25 * surface_temp) - remapped[1])
    heat_flux = 0.3 * wind_speed * (remapped[0] - surface_temp) - 1.5 * evaporation
    salt_flux = 0.5 * evaporation * (1.0 + 0.2 * surface_salt)
    return sea_state.at[0, 0].add(heat_flux).at[1, 0].add(salt_flux)


def body(
    atmos_state,
    ocean_state,
    level_weight,
    atmos_neighbors,
    atmos_diffusion,
    ocean_neighbors,
    ocean_diffusion,
    vertical_mixing,
    send_columns,
    read_slots,
    remap_weight,
):
    air_state = atmos_state
    air_block = air_state.shape[2]
    air_matrix = mixing_matrix(atmos_neighbors, atmos_diffusion, air_block + 2 * HALO, HALO)
    for substep in range(STEPS_ATM):
        padded = padded_2(air_state, ((("comp", "sub"), 2),), HALO)
        air_state = apply_mix(padded, air_matrix)
    partial_value = jnp.sum(level_weight[None, :, None] * air_state, axis=1)
    near_air = lax.psum(partial_value, "lev")
    positions = lax.axis_size(("comp", "sub"))
    capacity = send_columns.shape[0] // positions
    fields = near_air.shape[0]
    outgoing = jnp.take(near_air, send_columns, axis=1).reshape(fields, positions, capacity)
    incoming = lax.all_to_all(outgoing, ("comp", "sub"), split_axis=1, concat_axis=1, tiled=True)
    flat_rows = incoming.reshape(fields, positions * capacity)
    picked = jnp.take(flat_rows, read_slots, axis=1)
    remapped = jnp.sum(remap_weight * picked, axis=1) / jnp.sum(remap_weight, axis=0)
    sea_state = force(ocean_state, remapped)
    sea_block = sea_state.shape[2]
    sea_matrix = mixing_matrix(ocean_neighbors, ocean_diffusion, sea_block + 2 * HALO, HALO)
    for substep in range(STEPS_OCN):
        padded = padded_2(sea_state, ((("comp", "lev", "sub"), 2),), HALO)
        sea_state = vertical(apply_mix(padded, sea_matrix), vertical_mixing)
    return (air_state, sea_state)


def solution(mesh):
    in_specs = (
        P(None, "lev", ("member", "comp", "sub")),
        P(None, None, ("member", "comp", "lev", "sub")),
        P("lev"),
        P(None, ("comp", "sub")),
        P(None, ("comp", "sub")),
        P(None, ("comp", "lev", "sub")),
        P(None, ("comp", "lev", "sub")),
        P(("comp", "lev", "sub")),
        P(("comp", "lev", "sub")),
        P(None, ("comp", "lev", "sub")),
        P(None, ("comp", "lev", "sub")),
    )
    out_specs = (
        P(None, "lev", ("member", "comp", "sub")),
        P(None, None, ("member", "comp", "lev", "sub")),
    )
    return jax.shard_map(body, mesh=mesh, in_specs=in_specs, out_specs=out_specs, check_vma=False)
```

profile of v0, /device:TPU:0, one launch (start us, length us, event | category | flops | bytes accessed | tf_op | source)
XLA Modules:
  0.0 78.9 jit_solution(8218307833564969542)
XLA Ops:
  0.6 0.0 copy-start.5
  0.6 0.0 copy-start.6
  0.7 0.0 copy-start.2
  0.7 0.0 copy-start.7
  0.7 0.0 copy-start.3
  0.7 1.1 %copy.28 = f32[4,36,512]{2,1,0:T(8,128)S(1)} copy(f32[4,36,512]{2,0,1:T(4,128)} %param.15) | data formatting | bytes 589824 | tf_op args[0]
  1.8 0.1 fusion.70
  1.9 0.5 collective-permute-start
  2.4 4.1 %collective-permute-start.1 = (f32[4,36,64]{2,1,0:T(8,128)S(1)}, f32[4,36,64]{2,1,0:T(8,128)S(1)}, u32[]{:S(2)}, u32[]{:S(2)}) collective-permute-start(f32[4,36,64]{2,1,0:T(8,128)S(1)} %get-tuple-element.43), channel_id=1, source_target_pairs={{1,0},{4,1},{5,4},{8,5},{9,8},{12,9},{13,12},{0,13},{3,2},{6,3},{7... | collective-permute-start | bytes 110600 | tf_op jit(solution)/shard_map/ppermute | solution.py:19
  6.5 0.0 copy-done.5
  6.6 1.9 %collective-permute-done = f32[4,36,64]{2,1,0:T(8,128)S(1)} collective-permute-done((f32[4,36,64]{2,1,0:T(8,128)S(1)}, f32[4,36,64]{2,1,0:T(8,128)S(1)}, u32[]{:S(2)}, u32[]{:S(2)}) %collective-permute-start) | collective-permute-done | bytes 36896 | tf_op jit(solution)/shard_map/ppermute | solution.py:18
  8.6 0.0 collective-permute-done.1
  8.6 1.9 %fusion.6 = f32[4,36,512]{2,1,0:T(8,128)S(1)} fusion(f32[512]{0:T(512)S(1)} %broadcast_subtract_fusion, s32[512]{0:T(512)S(1)} %iota_add_fusion, f32[512]{0:T(512)S(1)} %bitcast.104, s32[512]{0:T(512)S(1)} %bitcast.84, f32[512]{0:T(512)S(1)} %bitcast.96, s32[512]{0:T(512)S(1)} %bitcast.88, f32[512]{0:T(512)S(1)} %bitcast.100, s32[512]{0:T(512)S(1)} %bitcast.80, ...), kind=kOutput, calls=%fused_computation.8 | convolution fusion | flops 571002880 | bytes 684032 | tf_op jit(solution)/shard_map/dot_general | solution.py:41
  10.4 0.1 fusion.69
  10.5 0.7 collective-permute-start.2
  11.2 3.0 %collective-permute-start.3 = (f32[4,36,64]{2,1,0:T(8,128)S(1)}, f32[4,36,64]{2,1,0:T(8,128)S(1)}, u32[]{:S(2)}, u32[]{:S(2)}) collective-permute-start(f32[4,36,64]{2,1,0:T(8,128)S(1)} %get-tuple-element.41), channel_id=1, source_target_pairs={{1,0},{4,1},{5,4},{8,5},{9,8},{12,9},{13,12},{0,13},{3,2},{6,3},{7... | collective-permute-start | bytes 110600 | tf_op jit(solution)/shard_map/ppermute | solution.py:19
  14.2 2.2 %collective-permute-done.2 = f32[4,36,64]{2,1,0:T(8,128)S(1)} collective-permute-done((f32[4,36,64]{2,1,0:T(8,128)S(1)}, f32[4,36,64]{2,1,0:T(8,128)S(1)}, u32[]{:S(2)}, u32[]{:S(2)}) %collective-permute-start.2) | collective-permute-done | bytes 36896 | tf_op jit(solution)/shard_map/ppermute | solution.py:18
  16.4 0.0 collective-permute-done.3
  16.4 1.9 %fusion.4 = f32[4,36,512]{2,1,0:T(8,128)S(1)} fusion(f32[512]{0:T(512)S(1)} %broadcast_subtract_fusion, s32[512]{0:T(512)S(1)} %iota_add_fusion, f32[512]{0:T(512)S(1)} %bitcast.105, s32[512]{0:T(512)S(1)} %bitcast.85, f32[512]{0:T(512)S(1)} %bitcast.97, s32[512]{0:T(512)S(1)} %bitcast.89, f32[512]{0:T(512)S(1)} %bitcast.101, s32[512]{0:T(512)S(1)} %bitcast.81, ...), kind=kOutput, calls=%fused_computation.6 | convolution fusion | flops 571002880 | bytes 684032 | tf_op jit(solution)/shard_map/dot_general | solution.py:41
  18.2 0.1 fusion.68
  18.3 0.1 collective-permute-start.4
  18.4 3.5 %collective-permute-start.5 = (f32[4,36,64]{2,1,0:T(8,128)S(1)}, f32[4,36,64]{2,1,0:T(8,128)S(1)}, u32[]{:S(2)}, u32[]{:S(2)}) collective-permute-start(f32[4,36,64]{2,1,0:T(8,128)S(1)} %get-tuple-element.39), channel_id=1, source_target_pairs={{1,0},{4,1},{5,4},{8,5},{9,8},{12,9},{13,12},{0,13},{3,2},{6,3},{7... | collective-permute-start | bytes 110600 | tf_op jit(solution)/shard_map/ppermute | solution.py:19
  21.9 2.4 %collective-permute-done.4 = f32[4,36,64]{2,1,0:T(8,128)S(1)} collective-permute-done((f32[4,36,64]{2,1,0:T(8,128)S(1)}, f32[4,36,64]{2,1,0:T(8,128)S(1)}, u32[]{:S(2)}, u32[]{:S(2)}) %collective-permute-start.4) | collective-permute-done | bytes 36896 | tf_op jit(solution)/shard_map/ppermute | solution.py:18
  24.3 0.0 collective-permute-done.5
  24.3 1.9 %fusion.2 = f32[4,36,512]{2,1,0:T(8,128)S(1)} fusion(f32[512]{0:T(512)S(1)} %broadcast_subtract_fusion, s32[512]{0:T(512)S(1)} %iota_add_fusion, f32[512]{0:T(512)S(1)} %bitcast.106, s32[512]{0:T(512)S(1)} %bitcast.86, f32[512]{0:T(512)S(1)} %bitcast.98, s32[512]{0:T(512)S(1)} %bitcast.90, f32[512]{0:T(512)S(1)} %bitcast.102, s32[512]{0:T(512)S(1)} %bitcast.82, ...), kind=kOutput, calls=%fused_computation.4 | convolution fusion | flops 571002880 | bytes 684032 | tf_op jit(solution)/shard_map/dot_general | solution.py:41
  26.2 0.1 fusion.67
  26.3 0.1 collective-permute-start.6
  26.3 3.5 %collective-permute-start.7 = (f32[4,36,64]{2,1,0:T(8,128)S(1)}, f32[4,36,64]{2,1,0:T(8,128)S(1)}, u32[]{:S(2)}, u32[]{:S(2)}) collective-permute-start(f32[4,36,64]{2,1,0:T(8,128)S(1)} %get-tuple-element.37), channel_id=1, source_target_pairs={{1,0},{4,1},{5,4},{8,5},{9,8},{12,9},{13,12},{0,13},{3,2},{6,3},{7... | collective-permute-start | bytes 110600 | tf_op jit(solution)/shard_map/ppermute | solution.py:19
  29.9 0.1 broadcast_in_dim.152
  30.0 2.6 %collective-permute-done.6 = f32[4,36,64]{2,1,0:T(8,128)S(1)} collective-permute-done((f32[4,36,64]{2,1,0:T(8,128)S(1)}, f32[4,36,64]{2,1,0:T(8,128)S(1)}, u32[]{:S(2)}, u32[]{:S(2)}) %collective-permute-start.6) | collective-permute-done | bytes 36896 | tf_op jit(solution)/shard_map/ppermute | solution.py:18
  32.6 0.0 collective-permute-done.7
  32.6 1.9 %multiply_reduce_fusion.1 = (f32[4,512]{1,0:T(4,128)S(1)}, f32[4,36,512]{2,1,0:T(8,128)S(1)}) fusion(f32[36]{0:T(128)S(1)} %copy-done.10, f32[512]{0:T(512)S(1)} %broadcast_subtract_fusion, s32[512]{0:T(512)S(1)} %iota_add_fusion, f32[512]{0:T(512)S(1)} %bitcast.107, s32[512]{0:T(512)S(1)} %bitcast.87, f32[512]{0:T(512)S(1)} %bitcast.99, ...), kind=kOutput, calls=%fused_computation.49 | convolution fusion | flops 571148288 | bytes 692368 | tf_op jit(solution)/shard_map/dot_general | solution.py:41
  34.4 0.0 copy-start.4
  34.5 0.1 copy.31
  34.6 11.9 %psum.7 = f32[4,512]{0,1:T(8,128)S(1)} all-reduce(f32[4,512]{0,1:T(8,128)S(1)} %copy.31), channel_id=1, replica_groups=mesh['member'=2,'comp'=4,'lev'=2,'sub'=2] {'lev'}, use_global_device_ids=true, to_apply=%region_2.3 | all-reduce | flops 2048 | bytes 16384 | tf_op jit(solution)/shard_map/psum | solution.py:83
  46.5 0.7 gather_fusion
  47.2 0.1 copy.32
  47.3 0.7 reshape.193
  48.0 4.0 %all-to-all-start = ((f32[8,1,128]{2,1,0:T(1,128)}), f32[8,1,128]{2,1,0:T(1,128)S(1)}, u32[]{:S(2)}, u32[]{:S(2)}) async-start(f32[8,1,128]{2,1,0:T(1,128)} %reshape.193), calls=%async_computation | async-start | bytes 8192 | tf_op jit(solution)/shard_map/all_to_all | solution.py:88
  52.1 5.4 %all-to-all-done = f32[8,1,128]{2,1,0:T(1,128)S(1)} async-done(((f32[8,1,128]{2,1,0:T(1,128)}), f32[8,1,128]{2,1,0:T(1,128)S(1)}, u32[]{:S(2)}, u32[]{:S(2)}) %all-to-all-start) | async-done | bytes 4128 | tf_op jit(solution)/shard_map/all_to_all | solution.py:88
  57.5 0.5 broadcast.152
  58.0 0.7 reduce.6
  58.7 0.1 reshape.194
  58.8 0.1 copy.33
  58.9 2.8 %gather_fusion.1 = f32[1024,4]{1,0:T(8,128)S(1)} fusion(f32[4,256]{0,1:T(8,128)S(1)} %bitcast.72, s32[1024]{0:T(1024)S(1)} %broadcast_clamp_fusion), kind=kCustom, calls=%fused_computation.1 | custom fusion | bytes 36864 | tf_op jit(solution)/shard_map/jit(_take)/gather | solution.py:90
  61.7 0.3 multiply_reduce_fusion
  62.1 0.1 copy.34
  62.1 0.0 copy-done
  62.3 0.1 fusion.76
  62.4 0.1 collective-permute-start.8
  62.5 4.4 %collective-permute-start.9 = (f32[2,80,64]{2,1,0:T(8,128)S(1)}, f32[2,80,64]{2,1,0:T(8,128)S(1)}, u32[]{:S(2)}, u32[]{:S(2)}) collective-permute-start(f32[2,80,64]{2,1,0:T(8,128)S(1)} %get-tuple-element.55), channel_id=1, source_target_pairs={{1,0},{2,1},{3,2},{4,3},{5,4},{6,5},{7,6},{8,7},{9,8},{10,9},{11,1... | collective-permute-start | bytes 122888 | tf_op jit(solution)/shard_map/ppermute | solution.py:19
  66.9 2.1 %collective-permute-done.8 = f32[2,80,64]{2,1,0:T(8,128)S(1)} collective-permute-done((f32[2,80,64]{2,1,0:T(8,128)S(1)}, f32[2,80,64]{2,1,0:T(8,128)S(1)}, u32[]{:S(2)}, u32[]{:S(2)}) %collective-permute-start.8) | collective-permute-done | bytes 40992 | tf_op jit(solution)/shard_map/ppermute | solution.py:18
  69.0 0.0 collective-permute-done.9
  69.0 0.8 fusion.30
  69.8 0.0 copy-start.8
  69.9 0.6 copy-done.8
  70.5 0.1 fusion.73
  70.6 0.1 collective-permute-start.10
  70.7 4.6 %collective-permute-start.11 = (f32[2,80,64]{2,1,0:T(8,128)S(1)}, f32[2,80,64]{2,1,0:T(8,128)S(1)}, u32[]{:S(2)}, u32[]{:S(2)}) collective-permute-start(f32[2,80,64]{2,1,0:T(8,128)S(1)} %get-tuple-element.49), channel_id=1, source_target_pairs={{1,0},{2,1},{3,2},{4,3},{5,4},{6,5},{7,6},{8,7},{9,8},{10,9},{11,1... | collective-permute-start | bytes 122888 | tf_op jit(solution)/shard_map/ppermute | solution.py:19
  75.3 0.9 %copy.35 = f32[4,36,512]{2,0,1:T(4,128)} copy(f32[4,36,512]{2,1,0:T(8,128)S(1)} %get-tuple-element.77) | data formatting | bytes 589824
  76.2 1.2 %collective-permute-done.10 = f32[2,80,64]{2,1,0:T(8,128)S(1)} collective-permute-done((f32[2,80,64]{2,1,0:T(8,128)S(1)}, f32[2,80,64]{2,1,0:T(8,128)S(1)}, u32[]{:S(2)}, u32[]{:S(2)}) %collective-permute-start.10) | collective-permute-done | bytes 40992 | tf_op jit(solution)/shard_map/ppermute | solution.py:18
  77.3 0.0 collective-permute-done.11
  77.3 0.8 fusion.28
  78.2 0.7 fusion.47
  (41 shorter events, 0.4 us)
Async XLA Ops:
  0.6 5.8 %copy-start.5 = (s32[4,256]{1,0:T(4,128)S(1)}, s32[4,256]{1,0:T(4,128)}, u32[]{:S(2)}) copy-start(s32[4,256]{1,0:T(4,128)} %param.24) | copy-start | bytes 12292
  0.6 5.8 %copy-start.6 = (s32[4,512]{1,0:T(4,128)S(1)}, s32[4,512]{1,0:T(4,128)}, u32[]{:S(2)}) copy-start(s32[4,512]{1,0:T(4,128)} %param.18) | copy-start | bytes 24580
  0.7 5.9 %copy-start.2 = (f32[4,512]{1,0:T(4,128)S(1)}, f32[4,512]{1,0:T(4,128)}, u32[]{:S(2)}) copy-start(f32[4,512]{1,0:T(4,128)} %param.19) | copy-start | bytes 24580
  0.7 5.9 %copy-start.7 = (s32[6,256]{1,0:T(8,128)S(1)}, s32[6,256]{1,0:T(8,128)}, u32[]{:S(2)}) copy-start(s32[6,256]{1,0:T(8,128)} %param.20) | copy-start | bytes 18436
  0.7 5.9 %copy-start.3 = (f32[6,256]{1,0:T(8,128)S(1)}, f32[6,256]{1,0:T(8,128)}, u32[]{:S(2)}) copy-start(f32[6,256]{1,0:T(8,128)} %param.21) | copy-start | bytes 18436
  1.9 6.7 %collective-permute-start = (f32[4,36,64]{2,1,0:T(8,128)S(1)}, f32[4,36,64]{2,1,0:T(8,128)S(1)}, u32[]{:S(2)}, u32[]{:S(2)}) collective-permute-start(f32[4,36,64]{2,1,0:T(8,128)S(1)} %get-tuple-element.42), channel_id=1, source_target_pairs={{0,1},{1,4},{4,5},{5,8},{8,9},{9,12},{12,13},{13,0},{2,3},{3,6},{6... | collective-permute-start | bytes 110600 | tf_op jit(solution)/shard_map/ppermute | solution.py:18
  2.4 6.2 %collective-permute-start.1 = (f32[4,36,64]{2,1,0:T(8,128)S(1)}, f32[4,36,64]{2,1,0:T(8,128)S(1)}, u32[]{:S(2)}, u32[]{:S(2)}) collective-permute-start(f32[4,36,64]{2,1,0:T(8,128)S(1)} %get-tuple-element.43), channel_id=1, source_target_pairs={{1,0},{4,1},{5,4},{8,5},{9,8},{12,9},{13,12},{0,13},{3,2},{6,3},{7... | collective-permute-start | bytes 110600 | tf_op jit(solution)/shard_map/ppermute | solution.py:19
  8.6 5.6 %copy-start.9 = (s32[256]{0:T(256)S(1)}, s32[256]{0:T(256)}, u32[]{:S(2)}) copy-start(s32[256]{0:T(256)} %param.23) | copy-start | bytes 3076
  10.5 5.9 %collective-permute-start.2 = (f32[4,36,64]{2,1,0:T(8,128)S(1)}, f32[4,36,64]{2,1,0:T(8,128)S(1)}, u32[]{:S(2)}, u32[]{:S(2)}) collective-permute-start(f32[4,36,64]{2,1,0:T(8,128)S(1)} %get-tuple-element.40), channel_id=1, source_target_pairs={{0,1},{1,4},{4,5},{5,8},{8,9},{9,12},{12,13},{13,0},{2,3},{3,6},{6... | collective-permute-start | bytes 110600 | tf_op jit(solution)/shard_map/ppermute | solution.py:18
  11.2 5.2 %collective-permute-start.3 = (f32[4,36,64]{2,1,0:T(8,128)S(1)}, f32[4,36,64]{2,1,0:T(8,128)S(1)}, u32[]{:S(2)}, u32[]{:S(2)}) collective-permute-start(f32[4,36,64]{2,1,0:T(8,128)S(1)} %get-tuple-element.41), channel_id=1, source_target_pairs={{1,0},{4,1},{5,4},{8,5},{9,8},{12,9},{13,12},{0,13},{3,2},{6,3},{7... | collective-permute-start | bytes 110600 | tf_op jit(solution)/shard_map/ppermute | solution.py:19
  18.3 6.0 %collective-permute-start.4 = (f32[4,36,64]{2,1,0:T(8,128)S(1)}, f32[4,36,64]{2,1,0:T(8,128)S(1)}, u32[]{:S(2)}, u32[]{:S(2)}) collective-permute-start(f32[4,36,64]{2,1,0:T(8,128)S(1)} %get-tuple-element.38), channel_id=1, source_target_pairs={{0,1},{1,4},{4,5},{5,8},{8,9},{9,12},{12,13},{13,0},{2,3},{3,6},{6... | collective-permute-start | bytes 110600 | tf_op jit(solution)/shard_map/ppermute | solution.py:18
  18.4 6.0 %collective-permute-start.5 = (f32[4,36,64]{2,1,0:T(8,128)S(1)}, f32[4,36,64]{2,1,0:T(8,128)S(1)}, u32[]{:S(2)}, u32[]{:S(2)}) collective-permute-start(f32[4,36,64]{2,1,0:T(8,128)S(1)} %get-tuple-element.39), channel_id=1, source_target_pairs={{1,0},{4,1},{5,4},{8,5},{9,8},{12,9},{13,12},{0,13},{3,2},{6,3},{7... | collective-permute-start | bytes 110600 | tf_op jit(solution)/shard_map/ppermute | solution.py:19
  21.9 10.6 %copy-start.10 = (f32[36]{0:T(128)S(1)}, f32[36]{0:T(128)}, u32[]{:S(2)}) copy-start(f32[36]{0:T(128)} %param.17) | copy-start | bytes 436
  26.3 6.3 %collective-permute-start.6 = (f32[4,36,64]{2,1,0:T(8,128)S(1)}, f32[4,36,64]{2,1,0:T(8,128)S(1)}, u32[]{:S(2)}, u32[]{:S(2)}) collective-permute-start(f32[4,36,64]{2,1,0:T(8,128)S(1)} %get-tuple-element.36), channel_id=1, source_target_pairs={{0,1},{1,4},{4,5},{5,8},{8,9},{9,12},{12,13},{13,0},{2,3},{3,6},{6... | collective-permute-start | bytes 110600 | tf_op jit(solution)/shard_map/ppermute | solution.py:18
  26.3 6.2 %collective-permute-start.7 = (f32[4,36,64]{2,1,0:T(8,128)S(1)}, f32[4,36,64]{2,1,0:T(8,128)S(1)}, u32[]{:S(2)}, u32[]{:S(2)}) collective-permute-start(f32[4,36,64]{2,1,0:T(8,128)S(1)} %get-tuple-element.37), channel_id=1, source_target_pairs={{1,0},{4,1},{5,4},{8,5},{9,8},{12,9},{13,12},{0,13},{3,2},{6,3},{7... | collective-permute-start | bytes 110600 | tf_op jit(solution)/shard_map/ppermute | solution.py:19
  34.4 17.6 %copy-start.4 = (f32[4,256]{1,0:T(4,128)S(1)}, f32[4,256]{1,0:T(4,128)}, u32[]{:S(2)}) copy-start(f32[4,256]{1,0:T(4,128)} %param.25) | copy-start | bytes 12292
  48.0 9.5 %all-to-all-start = ((f32[8,1,128]{2,1,0:T(1,128)}), f32[8,1,128]{2,1,0:T(1,128)S(1)}, u32[]{:S(2)}, u32[]{:S(2)}) async-start(f32[8,1,128]{2,1,0:T(1,128)} %reshape.193), calls=%async_computation | async-start | bytes 8192 | tf_op jit(solution)/shard_map/all_to_all | solution.py:88
  58.8 3.4 %copy-start = (f32[2,80,256]{2,1,0:T(8,128)S(1)}, f32[2,80,256]{2,1,0:T(8,128)}, u32[]{:S(2)}) copy-start(f32[2,80,256]{2,1,0:T(8,128)} %param.16) | copy-start | bytes 491524
  58.8 3.4 %copy-start.1 = (f32[2,80,256]{2,1,0:T(8,128)S(1)}, f32[2,80,256]{2,1,0:T(8,128)}, u32[]{:S(2)}) copy-start(f32[2,80,256]{2,1,0:T(8,128)} %param.16) | copy-start | bytes 491524
  62.4 6.6 %collective-permute-start.8 = (f32[2,80,64]{2,1,0:T(8,128)S(1)}, f32[2,80,64]{2,1,0:T(8,128)S(1)}, u32[]{:S(2)}, u32[]{:S(2)}) collective-permute-start(f32[2,80,64]{2,1,0:T(8,128)S(1)} %get-tuple-element.54), channel_id=1, source_target_pairs={{0,1},{1,2},{2,3},{3,4},{4,5},{5,6},{6,7},{7,8},{8,9},{9,10},{10,1... | collective-permute-start | bytes 122888 | tf_op jit(solution)/shard_map/ppermute | solution.py:18
  62.5 6.6 %collective-permute-start.9 = (f32[2,80,64]{2,1,0:T(8,128)S(1)}, f32[2,80,64]{2,1,0:T(8,128)S(1)}, u32[]{:S(2)}, u32[]{:S(2)}) collective-permute-start(f32[2,80,64]{2,1,0:T(8,128)S(1)} %get-tuple-element.55), channel_id=1, source_target_pairs={{1,0},{2,1},{3,2},{4,3},{5,4},{6,5},{7,6},{8,7},{9,8},{10,9},{11,1... | collective-permute-start | bytes 122888 | tf_op jit(solution)/shard_map/ppermute | solution.py:19
  69.8 0.7 copy-start.8
  70.6 6.7 %collective-permute-start.10 = (f32[2,80,64]{2,1,0:T(8,128)S(1)}, f32[2,80,64]{2,1,0:T(8,128)S(1)}, u32[]{:S(2)}, u32[]{:S(2)}) collective-permute-start(f32[2,80,64]{2,1,0:T(8,128)S(1)} %get-tuple-element.48), channel_id=1, source_target_pairs={{0,1},{1,2},{2,3},{3,4},{4,5},{5,6},{6,7},{7,8},{8,9},{9,10},{10,1... | collective-permute-start | bytes 122888 | tf_op jit(solution)/shard_map/ppermute | solution.py:18
  70.7 6.7 %collective-permute-start.11 = (f32[2,80,64]{2,1,0:T(8,128)S(1)}, f32[2,80,64]{2,1,0:T(8,128)S(1)}, u32[]{:S(2)}, u32[]{:S(2)}) collective-permute-start(f32[2,80,64]{2,1,0:T(8,128)S(1)} %get-tuple-element.49), channel_id=1, source_target_pairs={{1,0},{2,1},{3,2},{4,3},{5,4},{6,5},{7,6},{8,7},{9,8},{10,9},{11,1... | collective-permute-start | bytes 122888 | tf_op jit(solution)/shard_map/ppermute | solution.py:19
where the time goes:
time: 79.1 us; the launch traced here: 78.9 us
  starting transfers between devices  28.6 us (36%)
  waiting for transfers between devices  17.8 us (23%)
  blocking collectives  11.9 us (15%)
  matrix products  9 us (11%)
  local copies, waits for them, and re-layouts  8.7 us (11%)
  other arithmetic  1.92 us (2%)
  between operations  1.02 us (1%)
    ppermute x6, starting transfers between devices, padded_2(): after = lax.ppermute(initial, axis, down)  23.2 us
    ppermute x6, waiting for transfers between devices, padded_2(): before = lax.ppermute(last, axis, up)  12.3 us
    psum x1, blocking collectives, body(): near_air = lax.psum(partial_value, 'lev')  11.9 us
    dot_general x6, matrix products, apply_mix(): jnp.dot(flat, matrix, precision=lax.Precision.HIGHEST, preferred_element_...  9 us
    all_to_all x1, waiting for transfers between devices, body(): lax.all_to_all(outgoing, ('comp', 'sub'), split_axis=1, concat_axis=1, ti...  5.45 us
    all_to_all x1, starting transfers between devices, body(): lax.all_to_all(outgoing, ('comp', 'sub'), split_axis=1, concat_axis=1, ti...  3.99 us
    unnamed x27, local copies, waits for them, and re-layouts  3.43 us
    gather x1, local copies, waits for them, and re-layouts, body(): picked = jnp.take(flat_rows, read_slots, axis=1)  2.8 us
  transfers between devices with their start and end apart: 13, of which 7 were waited for; matrix products, arithmetic and copies ran while one was open for 1% of the time, Pallas kernels for 0%

commit v1 on v0

v1 whole, which is shorter than its diff:
```python
import functools

import jax
import jax.numpy as jnp
from jax import lax
from jax.experimental import pallas as pl
from jax.experimental.pallas import tpu as pltpu
from jax.sharding import PartitionSpec as P

HALO = 64
STEPS_ATM = 4
STEPS_OCN = 2
LANE = 128
MESH = pl.DeviceIdType.MESH


def pick(x, lanes):
    return jnp.take_along_axis(x, lanes, axis=1, mode="promise_in_bounds")


def lane_of(shape):
    return lax.broadcasted_iota(jnp.int32, shape, 1)


def mix_tile(first, second, places, rates, keep):
    shape = first.shape
    own = jnp.where(
        lane_of(shape) < HALO,
        pltpu.roll(first, HALO, axis=1),
        pltpu.roll(second, HALO, axis=1),
    )
    acc = keep * own
    for n in range(places.shape[0]):
        place = jnp.broadcast_to(places[n : n + 1], shape)
        lanes = jnp.bitwise_and(place, LANE - 1)
        value = jnp.where(place < LANE, pick(first, lanes), pick(second, lanes))
        acc = acc + rates[n : n + 1] * value
    return acc


def kernel(
    npos,
    nlev,
    air_hbm,
    sea_hbm,
    weight_ref,
    anb_ref,
    adf_ref,
    onb_ref,
    odf_ref,
    vm_ref,
    send_ref,
    slot_ref,
    rw_ref,
    air_out,
    sea_out,
    x0,
    xa,
    xb,
    y0,
    ya,
    rbuf,
    qbuf,
    aplace,
    arate,
    oplace,
    orate,
    table,
    pout,
    pin,
    flux,
    loc_sem,
    avg_send,
    avg_recv,
    tab_send,
    tab_recv,
    air_send,
    air_recv,
    sea_send,
    sea_recv,
    q_send,
    q_recv,
    route_send,
    route_recv,
):
    c, l, s = lax.axis_index("comp"), lax.axis_index("lev"), lax.axis_index("sub")
    ncomp = npos // 2
    d = 2 * c + s
    flds, levs, block = air_hbm.shape
    rim = STEPS_ATM * HALO
    cells = sea_hbm.shape[2]
    orim = STEPS_OCN * HALO
    cap = send_ref.shape[1] // npos
    nba, nbo, krem = anb_ref.shape[0], onb_ref.shape[0], slot_ref.shape[0]

    def at(pos, lev):
        pos = lax.rem(pos + npos, npos)
        return {"comp": pos // 2, "lev": lax.rem(lev + nlev, nlev), "sub": lax.rem(pos, 2)}

    def sea_at(step):
        g = lax.rem((c * nlev + l) * 2 + s + step + 2 * ncomp * nlev, 2 * ncomp * nlev)
        return {"comp": g // (2 * nlev), "lev": lax.rem(g // 2, nlev), "sub": lax.rem(g, 2)}

    load_air = pltpu.make_async_copy(air_hbm, x0.at[:, :, rim : rim + block], loc_sem.at[0])
    load_sea = pltpu.make_async_copy(sea_hbm, y0.at[:, :, orim : orim + cells], loc_sem.at[1])
    load_air.start()
    load_sea.start()

    barrier = pltpu.get_barrier_semaphore()
    for k in range(1, npos):
        pl.semaphore_signal(barrier, inc=1, device_id=at(d + k, l), device_id_type=MESH)
    for j in range(1, nlev):
        for w in (-1, 0, 1):
            pl.semaphore_signal(barrier, inc=1, device_id=at(d + w, l + j), device_id_type=MESH)

    def offsets(ref):
        places = ref[...]
        return (places - HALO - lane_of(places.shape)).astype(jnp.float32)

    own = slice(rim, rim + block)
    rbuf[0, 4 : 4 + nba, own] = adf_ref[...]
    rbuf[0, 8 : 8 + nba, own] = offsets(anb_ref)
    rbuf[0, 12:16, own] = jnp.zeros((4, block), jnp.float32)
    sea_own = slice(orim, orim + cells)
    qbuf[0:nbo, sea_own] = offsets(onb_ref)
    qbuf[6 : 6 + nbo, sea_own] = odf_ref[...]
    qbuf[12:13, sea_own] = vm_ref[...]
    qbuf[13 : 13 + krem, sea_own] = slot_ref[...].astype(jnp.float32)
    qbuf[17 : 17 + krem, sea_own] = rw_ref[...]
    qbuf[21:24, sea_own] = jnp.zeros((3, cells), jnp.float32)
    table[0] = jnp.broadcast_to(send_ref[...], table.shape[1:])

    load_air.wait()
    weight = weight_ref[...]
    for f in range(flds):
        rbuf[0, f : f + 1, own] = jnp.sum(weight * x0[f, :, own], axis=0, keepdims=True)
    load_sea.wait()

    pl.semaphore_wait(barrier, npos - 1 + 3 * (nlev - 1))

    def remote(src, dst, send, recv, device):
        return pltpu.make_async_remote_copy(
            src_ref=src, dst_ref=dst, send_sem=send, recv_sem=recv,
            device_id=device, device_id_type=MESH,
        )

    copies = []
    avg = []
    lefts = slice(0, rim)
    rights = slice(rim + block, rim + block + rim)
    low = slice(rim, 2 * rim)
    high = slice(block, block + rim)
    for j in range(nlev):
        rel = (nlev - j) % nlev
        rows = slice(0, 16) if j == 0 else slice(0, 8)
        for w, (src, dst, step) in enumerate(((high, lefts, 1), (own, own, 0), (low, rights, -1))):
            if j == 0 and step == 0:
                continue
            avg.append(
                remote(
                    rbuf.at[0, rows, src], rbuf.at[rel, rows, dst],
                    avg_send.at[rel * 3 + w], avg_recv.at[rel * 3 + w], at(d + step, l + j),
                )
            )
    tabs = [remote(table.at[0], table.at[1], tab_send.at[0], tab_recv.at[0], at(d, l + 1))]
    if nlev > 2:
        tabs.append(remote(table.at[0], table.at[2], tab_send.at[1], tab_recv.at[1], at(d, l - 1)))
    q_high, q_left = slice(cells, cells + orim), slice(0, orim)
    q_low, q_right = slice(orim, 2 * orim), slice(orim + cells, orim + cells + orim)
    qs = [
        remote(qbuf.at[:, q_high], qbuf.at[:, q_left], q_send.at[0], q_recv.at[0], sea_at(1)),
        remote(qbuf.at[:, q_low], qbuf.at[:, q_right], q_send.at[1], q_recv.at[1], sea_at(-1)),
    ]
    seas = [
        remote(y0.at[:, :, q_high], y0.at[:, :, q_left], sea_send.at[0], sea_recv.at[0], sea_at(1)),
        remote(y0.at[:, :, q_low], y0.at[:, :, q_right], sea_send.at[1], sea_recv.at[1], sea_at(-1)),
    ]
    airs = [
        remote(x0.at[:, :, high], x0.at[:, :, lefts], air_send.at[0], air_recv.at[0], at(d + 1, l)),
        remote(x0.at[:, :, low], x0.at[:, :, rights], air_send.at[1], air_recv.at[1], at(d - 1, l)),
    ]
    for copy in avg + tabs + qs + seas + airs:
        copy.start()

    for copy in avg:
        copy.wait_recv()
    packed = rbuf[0]
    wide = packed.shape[1]
    for shift in range(2):
        moved = pltpu.roll(packed, wide - HALO, axis=1) if shift else packed
        rates = moved[4 : 4 + nba]
        tile_lane = jnp.bitwise_and(lane_of((nba, wide)), LANE - 1)
        aplace[shift, 0:nba] = moved[8 : 8 + nba].astype(jnp.int32) + tile_lane + HALO
        arate[shift, 0:nba] = rates
        arate[shift, nba : nba + 1] = 1.0 - jnp.sum(rates, axis=0, keepdims=True)

    def air_tile(k, t, first, second):
        shift, base = (1 - k % 2), (k + 1) // 2
        cols = slice((base + t) * LANE, (base + t + 1) * LANE)
        return mix_tile(
            first, second, aplace[shift, 0:nba, cols], arate[shift, 0:nba, cols],
            arate[shift, nba : nba + 1, cols],
        )

    total = rbuf[0, 0:8]
    for j in range(1, nlev):
        total = total + rbuf[j, 0:8]
    top = lax.broadcasted_iota(jnp.int32, (8, LANE), 0)
    tiles = []
    for t in range(wide // LANE):
        tile = total[:, t * LANE : (t + 1) * LANE]
        tiles.append(jnp.where(top < 4, tile, pltpu.roll(tile, 4, axis=0)))
    for k in range(STEPS_ATM):
        tiles = [air_tile(k, t, tiles[t], tiles[t + 1]) for t in range(len(tiles) - 1)]

    for copy in tabs:
        copy.wait_recv()
    lane8 = lane_of((8, LANE))
    per_tile = LANE // cap
    up_row = 2 if nlev > 2 else 1

    def request(pos):
        odd = lax.rem(pos, 2)
        forward = jnp.where(odd == 0, l > 0, l == nlev - 1)
        cross = lax.rem(pos + jnp.where(forward, 1, npos - 1), npos)
        start = pl.multiple_of(pos // per_tile * LANE, LANE)
        mine = table[0, :, pl.ds(start, LANE)]
        mine = pltpu.roll(mine, lax.rem(LANE - lax.rem(pos, per_tile) // 2 * 2 * cap, LANE), axis=1)
        start = pl.multiple_of(cross // per_tile * LANE, LANE)
        row = jnp.where(odd == 0, 1, up_row)
        other = table[row, :, pl.ds(start, LANE)]
        turn = lax.rem(2 * cap - lax.rem(cross, per_tile) * cap + LANE, LANE)
        other = pltpu.roll(other, turn, axis=1)
        column = jnp.where(lane8 < 2 * cap, mine, other)
        lanes = jnp.bitwise_and(column, LANE - 1)
        value = pick(tiles[0], lanes)
        for t in range(1, len(tiles)):
            value = jnp.where(column >= t * LANE, pick(tiles[t], lanes), value)
        return value

    routes = []
    for k in range(npos):
        pos = lax.rem(d + k, npos)
        if k == 0:
            pin[0] = request(pos)
            continue
        pout[k] = request(pos)
        copy = remote(pout.at[k], pin.at[k], route_send.at[k], route_recv.at[k], at(pos, l))
        copy.start()
        routes.append(copy)

    for copy in qs + seas:
        copy.wait_recv()
    qall = qbuf[...]
    qwide = qall.shape[1]
    for shift in range(2):
        moved = pltpu.roll(qall, qwide - HALO, axis=1) if shift else qall
        rates = moved[6 : 6 + nbo]
        tile_lane = jnp.bitwise_and(lane_of((nbo, qwide)), LANE - 1)
        oplace[shift, 0:nbo] = moved[0:nbo].astype(jnp.int32) + tile_lane + HALO
        orate[shift, 0:nbo] = rates
        orate[shift, nbo : nbo + 1] = 1.0 - jnp.sum(rates, axis=0, keepdims=True)
        orate[shift, nbo + 1 : nbo + 2] = moved[12:13]

    def sea_cols(k, t):
        base = (k + 1) // 2
        return 1 - k % 2, slice((base + t) * LANE, (base + t + 1) * LANE)

    def sea_tile(k, t, first, second):
        shift, cols = sea_cols(k, t)
        return mix_tile(
            first, second, oplace[shift, 0:nbo, cols], orate[shift, 0:nbo, cols],
            orate[shift, nbo : nbo + 1, cols],
        )

    def sea_vertical(k, t):
        shift, cols = sea_cols(k, t)
        return orate[shift, nbo + 1 : nbo + 2, cols]

    src = y0
    for k in range(STEPS_OCN):
        dst = sea_out if k == STEPS_OCN - 1 else ya

        def sea_step(tracer, carry, k=k, src=src, dst=dst):
            depth = src.shape[1]
            level = lax.broadcasted_iota(jnp.int32, (depth, LANE), 0)
            for t in range(dst.shape[2] // LANE):
                first = src[tracer, :, t * LANE : (t + 1) * LANE]
                second = src[tracer, :, (t + 1) * LANE : (t + 2) * LANE]
                v = sea_tile(k, t, first, second)
                up = jnp.where(level == 0, v, pltpu.roll(v, 1, axis=0))
                down = jnp.where(level == depth - 1, v, pltpu.roll(v, depth - 1, axis=0))
                v = v + sea_vertical(k, t) * (up - 2.0 * v + down)
                dst[tracer, :, t * LANE : (t + 1) * LANE] = v
            return carry

        lax.fori_loop(0, src.shape[0], sea_step, 0)
        src = dst

    for copy in airs:
        copy.wait_recv()
    src = x0
    for k in range(STEPS_ATM):
        dst = air_out if k == STEPS_ATM - 1 else (xa if k % 2 == 0 else xb)
        count = wide // LANE - 1 - k

        def air_step(f, carry, k=k, src=src, dst=dst, count=count):
            for t in range(count):
                first = src[f, :, t * LANE : (t + 1) * LANE]
                second = src[f, :, (t + 1) * LANE : (t + 2) * LANE]
                dst[f, :, t * LANE : (t + 1) * LANE] = air_tile(k, t, first, second)
            return carry

        lax.fori_loop(0, flds, air_step, 0)
        src = dst

    for copy in routes:
        copy.wait_recv()
    sub8 = lax.broadcasted_iota(jnp.int32, (8, LANE), 0)
    kinds = [jnp.where(s == 0, 2, 0)] + [s] * (cells // LANE) + [jnp.where(s == 0, 1, 2)]
    changes = []
    for t in range(qwide // LANE):
        cols = slice(t * LANE, (t + 1) * LANE)
        slots = qbuf[13 : 13 + krem, cols].astype(jnp.int32)
        weights = qbuf[17 : 17 + krem, cols]
        acc = jnp.zeros((8, LANE), jnp.float32)
        for m in range(krem // 2):
            m2 = m + krem // 2
            slot = jnp.where(sub8 < 4, slots[m : m + 1], slots[m2 : m2 + 1])
            weight2 = jnp.where(sub8 < 4, weights[m : m + 1], weights[m2 : m2 + 1])
            far = lax.rem(d - slot // cap + npos, npos)
            lanes = lax.rem(slot, cap) + kinds[t] * cap
            value = pick(pin[0], lanes)
            for k in range(1, npos):
                value = jnp.where(far == k, pick(pin[k], lanes), value)
            acc = acc + weight2 * value
        acc = acc + pltpu.roll(acc, 4, axis=0)
        acc = acc / jnp.sum(weights, axis=0, keepdims=True)
        temp, humid, east, north = (acc[i : i + 1] for i in range(4))
        sst = y0[0, 0:1, cols]
        salt = y0[1, 0:1, cols]
        wind = jnp.sqrt(east * east + north * north + 1.0)
        evap = 0.2 * wind * (0.5 * jnp.exp(0.25 * sst) - humid)
        heat = 0.3 * wind * (temp - sst) - 1.5 * evap
        brine = 0.5 * evap * (1.0 + 0.2 * salt)
        changes.append(jnp.where(sub8 == 0, heat, jnp.where(sub8 == 1, brine, 0.0)))
    later = []
    for t in range(len(changes) - 1):
        v = sea_tile(0, t, changes[t], changes[t + 1])
        mixing = sea_vertical(0, t)
        later.append(jnp.where(sub8 < 2, (1.0 - mixing) * v, mixing * pltpu.roll(v, 2, axis=0)))
    for t in range(len(later) - 1):
        v = sea_tile(1, t, later[t], later[t + 1])
        mixing = sea_vertical(1, t)
        cols = slice(t * LANE, (t + 1) * LANE)
        for tracer in range(2):
            a, b = v[tracer : tracer + 1], v[2 + tracer : 3 + tracer]
            sea_out[tracer, 0:1, cols] += a + mixing * (b - a)
            sea_out[tracer, 1:2, cols] += b + mixing * (a - 2.0 * b)
            sea_out[tracer, 2:3, cols] += mixing * b

    for copy in avg + tabs + qs + seas + airs + routes:
        copy.wait_send()


def body(
    npos,
    nlev,
    atmos_state,
    ocean_state,
    level_weight,
    atmos_neighbors,
    atmos_diffusion,
    ocean_neighbors,
    ocean_diffusion,
    vertical_mixing,
    send_columns,
    read_slots,
    remap_weight,
):
    flds, levs, block = atmos_state.shape
    tracers, depth, cells = ocean_state.shape
    wide = block + 2 * STEPS_ATM * HALO
    qwide = cells + 2 * STEPS_OCN * HALO
    vmem = pl.BlockSpec(memory_space=pltpu.VMEM)
    anywhere = pl.BlockSpec(memory_space=pl.ANY)
    dma = pltpu.SemaphoreType.DMA
    places = send_columns.shape[0]
    return pl.pallas_call(
        functools.partial(kernel, npos, nlev),
        out_shape=(
            jax.ShapeDtypeStruct(atmos_state.shape, jnp.float32),
            jax.ShapeDtypeStruct(ocean_state.shape, jnp.float32),
        ),
        in_specs=[anywhere] * 2 + [vmem] * 9,
        out_specs=(vmem, vmem),
        scratch_shapes=[
            pltpu.VMEM((flds, levs, wide), jnp.float32),
            pltpu.VMEM((flds, levs, wide - LANE), jnp.float32),
            pltpu.VMEM((flds, levs, wide - 2 * LANE), jnp.float32),
            pltpu.VMEM((tracers, depth, qwide), jnp.float32),
            pltpu.VMEM((tracers, depth, qwide - LANE), jnp.float32),
            pltpu.VMEM((nlev, 16, wide), jnp.float32),
            pltpu.VMEM((24, qwide), jnp.float32),
            pltpu.VMEM((2, 8, wide), jnp.int32),
            pltpu.VMEM((2, 8, wide), jnp.float32),
            pltpu.VMEM((2, 8, qwide), jnp.int32),
            pltpu.VMEM((2, 8, qwide), jnp.float32),
            pltpu.VMEM((3, 8, places), jnp.int32),
            pltpu.VMEM((npos, 8, LANE), jnp.float32),
            pltpu.VMEM((npos, 8, LANE), jnp.float32),
            pltpu.VMEM((8, LANE), jnp.float32),
            dma((2,)),
            dma((3 * nlev,)),
            dma((3 * nlev,)),
            dma((2,)),
            dma((2,)),
            dma((2,)),
            dma((2,)),
            dma((2,)),
            dma((2,)),
            dma((2,)),
            dma((2,)),
            dma((npos,)),
            dma((npos,)),
        ],
        compiler_params=pltpu.CompilerParams(
            collective_id=0, has_side_effects=True, vmem_limit_bytes=32 * 1024 * 1024
        ),
    )(
        atmos_state,
        ocean_state,
        level_weight[:, None],
        atmos_neighbors,
        atmos_diffusion,
        ocean_neighbors,
        ocean_diffusion,
        vertical_mixing[None, :],
        send_columns[None, :],
        read_slots,
        remap_weight,
    )


def solution(mesh):
    npos = mesh.shape["comp"] * mesh.shape["sub"]
    nlev = mesh.shape["lev"]
    in_specs = (
        P(None, "lev", ("member", "comp", "sub")),
        P(None, None, ("member", "comp", "lev", "sub")),
        P("lev"),
        P(None, ("comp", "sub")),
        P(None, ("comp", "sub")),
        P(None, ("comp", "lev", "sub")),
        P(None, ("comp", "lev", "sub")),
        P(("comp", "lev", "sub")),
        P(("comp", "lev", "sub")),
        P(None, ("comp", "lev", "sub")),
        P(None, ("comp", "lev", "sub")),
    )
    out_specs = (
        P(None, "lev", ("member", "comp", "sub")),
        P(None, None, ("member", "comp", "lev", "sub")),
    )
    return jax.shard_map(
        functools.partial(body, npos, nlev),
        mesh=mesh,
        in_specs=in_specs,
        out_specs=out_specs,
        check_vma=False,
    )
```

time: 79.1 us -> 25.3 us (0.32)
  starting transfers between devices: 28.6 us -> 0 us
  Pallas kernels: 0 us -> 20.8 us
  waiting for transfers between devices: 17.8 us -> 0 us
  blocking collectives: 11.9 us -> 0 us
  matrix products: 9 us -> 0 us
  local copies, waits for them, and re-layouts: 8.7 us -> 3.54 us
  other arithmetic: 1.92 us -> 0 us
    ppermute x12 -> x0, starting transfers between devices: 24.6 us -> none  [the longest x6 23.2 us: padded_2(): after = lax.ppermute(initial, axis, down)]
    pallas_call x0 -> x1, Pallas kernels: none -> 20.8 us  [body(): pl.pallas_call(functools.partial(kernel, npos, nlev), out_shape=(jax.Shap...]
    ppermute x12 -> x0, waiting for transfers between devices: 12.3 us -> none  [the longest x6 12.3 us: padded_2(): before = lax.ppermute(last, axis, up)]
    psum x1 -> x0, blocking collectives: 11.9 us -> none  [body(): near_air = lax.psum(partial_value, 'lev')]
    dot_general x6 -> x0, matrix products: 9 us -> none  [apply_mix(): jnp.dot(flat, matrix, precision=lax.Precision.HIGHEST, preferred_element_...]
    all_to_all x1 -> x0, waiting for transfers between devices: 5.45 us -> none  [body(): lax.all_to_all(outgoing, ('comp', 'sub'), split_axis=1, concat_axis=1, ti...]
    all_to_all x1 -> x0, starting transfers between devices: 3.99 us -> none  [body(): lax.all_to_all(outgoing, ('comp', 'sub'), split_axis=1, concat_axis=1, ti...]
    gather x3 -> x0, local copies, waits for them, and re-layouts: 3.64 us -> none  [the longest x1 2.8 us: body(): picked = jnp.take(flat_rows, read_slots, axis=1)]
  transfers between devices with their start and end apart: 13 -> 0, of which waited for: 7 -> 0; matrix products, arithmetic and copies ran while one was open for 1% -> 0% of each run, Pallas kernels for 0% -> 0%
where the time goes in v1:
time: 25.3 us; the launch traced here: 25.1 us
  Pallas kernels  20.8 us (82%)
  local copies, waits for them, and re-layouts  3.54 us (14%)
  between operations  0.77 us (3%)
    pallas_call x1, Pallas kernels, body(): pl.pallas_call(functools.partial(kernel, npos, nlev), out_shape=(jax.Shap...  20.8 us
    unnamed x22, local copies, waits for them, and re-layouts  2.53 us
    pallas_call x1, local copies, waits for them, and re-layouts, body(): pl.pallas_call(functools.partial(kernel, npos, nlev), out_shape=(jax.Shap...  0.91 us

profile of v1, /device:TPU:0, one launch (start us, length us, event | category | flops | bytes accessed | tf_op | source)
XLA Modules:
  0.0 25.1 jit_solution(1781691652415743769)
XLA Ops:
  0.6 0.0 copy-start.9
  0.6 0.6 %copy-done.9 = f32[36]{0:T(128)S(1)} copy-done((f32[36]{0:T(128)S(1)}, f32[36]{0:T(128)}, u32[]{:S(2)}) %copy-start.9) | copy-done | bytes 168
  1.3 0.1 copy.14.weight_ref
  1.4 0.0 copy-start
  1.4 0.0 copy-start.1
  1.4 0.0 copy-start.2
  1.4 0.0 copy-start.3
  1.4 0.0 copy-start.4
  1.4 0.0 copy-start.5
  1.4 0.0 copy-start.6
  1.4 0.0 copy-start.7
  1.5 0.0 copy-start.8
  1.5 1.2 %copy.13.air_hbm = f32[4,36,512]{2,1,0:T(8,128)S(1)} copy(f32[4,36,512]{2,0,1:T(4,128)} %param.11) | data formatting | bytes 589824 | tf_op args[0]
  2.6 0.0 copy-done
  2.6 0.0 copy-done.1
  2.7 0.0 copy-done.2
  2.7 0.0 copy-done.3
  2.7 0.0 copy-done.4
  2.7 0.0 copy-done.5
  2.7 0.0 copy-done.6
  2.7 0.0 copy-done.7
  2.7 0.0 copy-done.8
  2.7 20.8 %shard_map.122 = (f32[4,36,512]{2,1,0:T(8,128)S(1)}, f32[2,80,256]{2,1,0:T(8,128)S(1)}) custom-call(f32[4,36,512]{2,1,0:T(8,128)S(1)} %copy.13.air_hbm, f32[2,80,256]{2,1,0:T(8,128)S(1)} %copy-done, f32[36,1]{1,0:T(8,128)S(1)} %copy.14.weight_ref, s32[4,512]{1,0:T(4,128)S(1)} %copy-done.1, f32[4,512]{1,0:T(4,128)S(1)} %copy-done.2, s32[6,256]{1,0:T(8,128)S(1)} %copy-done.3, ...), custom_call_target="tpu_custom_call" | custom-call | tf_op jit(solution)/shard_map/pallas_call | solution.py:389
  23.5 0.9 %copy.15 = f32[4,36,512]{2,0,1:T(4,128)} copy(f32[4,36,512]{2,1,0:T(8,128)S(1)} %get-tuple-element.2) | data formatting | bytes 589824 | tf_op jit(solution)/shard_map/pallas_call | solution.py:389
  24.5 0.7 %copy.17 = f32[2,80,256]{2,1,0:T(8,128)} copy(f32[2,80,256]{2,1,0:T(8,128)S(1)} %get-tuple-element.7) | data formatting | bytes 327680
Async XLA Ops:
  0.6 0.7 %copy-start.9 = (f32[36]{0:T(128)S(1)}, f32[36]{0:T(128)}, u32[]{:S(2)}) copy-start(f32[36]{0:T(128)} %param.13) | copy-start | bytes 436
  1.4 1.3 %copy-start = (f32[2,80,256]{2,1,0:T(8,128)S(1)}, f32[2,80,256]{2,1,0:T(8,128)}, u32[]{:S(2)}) copy-start(f32[2,80,256]{2,1,0:T(8,128)} %sea_hbm.1) | copy-start | bytes 491524
  1.4 1.3 %copy-start.1 = (s32[4,512]{1,0:T(4,128)S(1)}, s32[4,512]{1,0:T(4,128)}, u32[]{:S(2)}) copy-start(s32[4,512]{1,0:T(4,128)} %anb_ref.1) | copy-start | bytes 24580
  1.4 1.3 %copy-start.2 = (f32[4,512]{1,0:T(4,128)S(1)}, f32[4,512]{1,0:T(4,128)}, u32[]{:S(2)}) copy-start(f32[4,512]{1,0:T(4,128)} %adf_ref.1) | copy-start | bytes 24580
  1.4 1.3 %copy-start.3 = (s32[6,256]{1,0:T(8,128)S(1)}, s32[6,256]{1,0:T(8,128)}, u32[]{:S(2)}) copy-start(s32[6,256]{1,0:T(8,128)} %onb_ref.1) | copy-start | bytes 18436
  1.4 1.3 %copy-start.4 = (f32[6,256]{1,0:T(8,128)S(1)}, f32[6,256]{1,0:T(8,128)}, u32[]{:S(2)}) copy-start(f32[6,256]{1,0:T(8,128)} %odf_ref.1) | copy-start | bytes 18436
  1.4 1.3 %copy-start.5 = (s32[4,256]{1,0:T(4,128)S(1)}, s32[4,256]{1,0:T(4,128)}, u32[]{:S(2)}) copy-start(s32[4,256]{1,0:T(4,128)} %slot_ref.1) | copy-start | bytes 12292
  1.4 1.3 %copy-start.6 = (f32[4,256]{1,0:T(4,128)S(1)}, f32[4,256]{1,0:T(4,128)}, u32[]{:S(2)}) copy-start(f32[4,256]{1,0:T(4,128)} %rw_ref.1) | copy-start | bytes 12292
  1.4 1.3 %copy-start.7 = (f32[256]{0:T(256)S(1)}, f32[256]{0:T(256)}, u32[]{:S(2)}) copy-start(f32[256]{0:T(256)} %param.18) | copy-start | bytes 3076
  1.5 1.3 %copy-start.8 = (s32[256]{0:T(256)S(1)}, s32[256]{0:T(256)}, u32[]{:S(2)}) copy-start(s32[256]{0:T(256)} %param.19) | copy-start | bytes 3076

commit v2 on v1

--- a/solution.py
+++ b/solution.py
@@ -43,6 +43,20 @@
     nlev,
     air_hbm,
     sea_hbm,
+    weight_hbm,
+    *rest,
+):
+    (
+    anb_hbm,
+    adf_hbm,
+    onb_hbm,
+    odf_hbm,
+    vm_hbm,
+    send_hbm,
+    slot_hbm,
+    rw_hbm,
+    air_out,
+    sea_out,
     weight_ref,
     anb_ref,
     adf_ref,
@@ -52,11 +66,11 @@
     send_ref,
     slot_ref,
     rw_ref,
-    air_out,
-    sea_out,
     x0,
+    xf,
     xa,
     xb,
+    mats,
     y0,
     ya,
     rbuf,
@@ -68,7 +82,6 @@
     table,
     pout,
     pin,
-    flux,
     loc_sem,
     avg_send,
     avg_recv,
@@ -82,11 +95,11 @@
     q_recv,
     route_send,
     route_recv,
-):
+    ) = rest
     c, l, s = lax.axis_index("comp"), lax.axis_index("lev"), lax.axis_index("sub")
     ncomp = npos // 2
     d = 2 * c + s
-    flds, levs, block = air_hbm.shape
+    levs, flds, block = air_hbm.shape
     rim = STEPS_ATM * HALO
     cells = sea_hbm.shape[2]
     orim = STEPS_OCN * HALO
@@ -100,11 +113,6 @@
     def sea_at(step):
         g = lax.rem((c * nlev + l) * 2 + s + step + 2 * ncomp * nlev, 2 * ncomp * nlev)
         return {"comp": g // (2 * nlev), "lev": lax.rem(g // 2, nlev), "sub": lax.rem(g, 2)}
-
-    load_air = pltpu.make_async_copy(air_hbm, x0.at[:, :, rim : rim + block], loc_sem.at[0])
-    load_sea = pltpu.make_async_copy(sea_hbm, y0.at[:, :, orim : orim + cells], loc_sem.at[1])
-    load_air.start()
-    load_sea.start()
 
     barrier = pltpu.get_barrier_semaphore()
     for k in range(1, npos):
@@ -112,6 +120,23 @@
     for j in range(1, nlev):
         for w in (-1, 0, 1):
             pl.semaphore_signal(barrier, inc=1, device_id=at(d + w, l + j), device_id_type=MESH)
+
+    load_air = pltpu.make_async_copy(air_hbm, x0.at[:, :, rim : rim + block], loc_sem.at[0])
+    load_sea = pltpu.make_async_copy(sea_hbm, y0.at[:, :, orim : orim + cells], loc_sem.at[1])
+    small = [
+        pltpu.make_async_copy(src, dst, loc_sem.at[2 + i])
+        for i, (src, dst) in enumerate((
+            (weight_hbm, weight_ref), (anb_hbm, anb_ref), (adf_hbm, adf_ref),
+            (send_hbm, send_ref), (onb_hbm, onb_ref), (odf_hbm, odf_ref), (vm_hbm, vm_ref),
+            (slot_hbm, slot_ref), (rw_hbm, rw_ref),
+        ))
+    ]
+    load_air.start()
+    for copy in small:
+        copy.start()
+    load_sea.start()
+    for copy in small:
+        copy.wait()
 
     def offsets(ref):
         places = ref[...]
@@ -131,9 +156,10 @@
     table[0] = jnp.broadcast_to(send_ref[...], table.shape[1:])
 
     load_air.wait()
-    weight = weight_ref[...]
-    for f in range(flds):
-        rbuf[0, f : f + 1, own] = jnp.sum(weight * x0[f, :, own], axis=0, keepdims=True)
+    sums = [weight_ref[k] * x0[k, :, own] for k in range(4)]
+    for k in range(4, levs):
+        sums[k % 4] = sums[k % 4] + weight_ref[k] * x0[k, :, own]
+    rbuf[0, 0:flds, own] = (sums[0] + sums[1]) + (sums[2] + sums[3])
     load_sea.wait()
 
     pl.semaphore_wait(barrier, npos - 1 + 3 * (nlev - 1))
@@ -182,17 +208,52 @@
     for copy in avg + tabs + qs + seas + airs:
         copy.start()
 
+    def tables(data, shift):
+        span = data.shape[1]
+        moved = pltpu.roll(data, span - HALO, axis=1) if shift else data
+        rates = moved[4 : 4 + nba]
+        tile_lane = jnp.bitwise_and(lane_of((nba, span)), LANE - 1)
+        places = moved[8 : 8 + nba].astype(jnp.int32) + tile_lane + HALO
+        return places, rates, 1.0 - jnp.sum(rates, axis=0, keepdims=True)
+
+    row_ids = lax.broadcasted_iota(jnp.int32, (2 * LANE, LANE), 0)
+    self_ids = lane_of((2 * LANE, LANE)) + HALO
+
+    def build(index, places, rates, keep):
+        matrix = jnp.where(row_ids == self_ids, keep, 0.0)
+        for n in range(nba):
+            matrix = matrix + jnp.where(row_ids == places[n : n + 1], rates[n : n + 1], 0.0)
+        upper = matrix.astype(jnp.bfloat16)
+        mats[index, :, 0:LANE] = upper
+        mats[index, :, LANE:] = (matrix - upper.astype(jnp.float32)).astype(jnp.bfloat16)
+
+    wide = rbuf.shape[2]
+    own_data = rbuf[0, :, own]
+    rim_tiles, block_tiles = rim // LANE, block // LANE
+    shifted_count = wide // LANE - 1
+    done = set()
+    for shift in range(2):
+        places, rates, keep = tables(own_data, shift)
+        for t in range(block_tiles - shift):
+            cols = slice(t * LANE, (t + 1) * LANE)
+            index = rim_tiles + t + (0 if shift else shifted_count - 1)
+            build(index, places[:, cols], rates[:, cols], keep[:, cols])
+            done.add(index)
+
+    def flatten(cols):
+        for k in range(0, levs, 2):
+            xf[4 * k : 4 * k + 8, cols] = jnp.concatenate([x0[k, :, cols], x0[k + 1, :, cols]], axis=0)
+
+    flatten(own)
+
     for copy in avg:
         copy.wait_recv()
     packed = rbuf[0]
-    wide = packed.shape[1]
     for shift in range(2):
-        moved = pltpu.roll(packed, wide - HALO, axis=1) if shift else packed
-        rates = moved[4 : 4 + nba]
-        tile_lane = jnp.bitwise_and(lane_of((nba, wide)), LANE - 1)
-        aplace[shift, 0:nba] = moved[8 : 8 + nba].astype(jnp.int32) + tile_lane + HALO
+        places, rates, keep = tables(packed, shift)
+        aplace[shift, 0:nba] = places
         arate[shift, 0:nba] = rates
-        arate[shift, nba : nba + 1] = 1.0 - jnp.sum(rates, axis=0, keepdims=True)
+        arate[shift, nba : nba + 1] = keep
 
     def air_tile(k, t, first, second):
         shift, base = (1 - k % 2), (k + 1) // 2
@@ -297,21 +358,40 @@
         lax.fori_loop(0, src.shape[0], sea_step, 0)
         src = dst
 
+    for shift in range(2):
+        for t in range(1 - shift, shifted_count):
+            index = t + (0 if shift else shifted_count - 1)
+            if index in done:
+                continue
+            cols = slice(t * LANE, (t + 1) * LANE)
+            build(
+                index, aplace[shift, 0:nba, cols], arate[shift, 0:nba, cols],
+                arate[shift, nba : nba + 1, cols],
+            )
     for copy in airs:
         copy.wait_recv()
-    src = x0
+    flatten(lefts)
+    flatten(rights)
+    rows = xf.shape[0]
+    src = xf
     for k in range(STEPS_ATM):
-        dst = air_out if k == STEPS_ATM - 1 else (xa if k % 2 == 0 else xb)
-        count = wide // LANE - 1 - k
-
-        def air_step(f, carry, k=k, src=src, dst=dst, count=count):
-            for t in range(count):
-                first = src[f, :, t * LANE : (t + 1) * LANE]
-                second = src[f, :, (t + 1) * LANE : (t + 2) * LANE]
-                dst[f, :, t * LANE : (t + 1) * LANE] = air_tile(k, t, first, second)
-            return carry
-
-        lax.fori_loop(0, flds, air_step, 0)
+        dst = xa if k % 2 == 0 else xb
+        for t in range(shifted_count - k):
+            shift, base = 1 - k % 2, (k + 1) // 2
+            index = base + t + (0 if shift else shifted_count - 1)
+            x = src[:, t * LANE : (t + 2) * LANE]
+            upper = x.astype(jnp.bfloat16)
+            lower = (x - upper.astype(jnp.float32)).astype(jnp.bfloat16)
+            both = jnp.concatenate([upper, lower], axis=0)
+            prod = jnp.dot(both, mats[index], preferred_element_type=jnp.float32)
+            small_part = prod[rows:, 0:LANE] + prod[:rows, LANE:] + prod[rows:, LANE:]
+            result = prod[:rows, 0:LANE] + small_part
+            cols = slice(t * LANE, (t + 1) * LANE)
+            if k < STEPS_ATM - 1:
+                dst[:, cols] = result
+            else:
+                for level in range(levs):
+                    air_out[level, :, cols] = result[4 * level : 4 * level + 4]
         src = dst
 
     for copy in routes:
@@ -382,45 +462,53 @@
     tracers, depth, cells = ocean_state.shape
     wide = block + 2 * STEPS_ATM * HALO
     qwide = cells + 2 * STEPS_OCN * HALO
+    rows = -(-flds * levs // 16) * 16
     vmem = pl.BlockSpec(memory_space=pltpu.VMEM)
-    anywhere = pl.BlockSpec(memory_space=pl.ANY)
+    hbm = pl.BlockSpec(memory_space=pltpu.HBM)
     dma = pltpu.SemaphoreType.DMA
+    f32, i32 = jnp.float32, jnp.int32
     places = send_columns.shape[0]
-    return pl.pallas_call(
+    small = (
+        (atmos_neighbors.shape, i32),
+        (atmos_diffusion.shape, f32),
+        (ocean_neighbors.shape, i32),
+        (ocean_diffusion.shape, f32),
+        ((1, cells), f32),
+        ((1, places), i32),
+        (read_slots.shape, i32),
+        (remap_weight.shape, f32),
+    )
+    air, sea = pl.pallas_call(
         functools.partial(kernel, npos, nlev),
         out_shape=(
-            jax.ShapeDtypeStruct(atmos_state.shape, jnp.float32),
-            jax.ShapeDtypeStruct(ocean_state.shape, jnp.float32),
+            jax.ShapeDtypeStruct((levs, flds, block), f32),
+            jax.ShapeDtypeStruct(ocean_state.shape, f32),
         ),
-        in_specs=[anywhere] * 2 + [vmem] * 9,
+        in_specs=[hbm] * 11,
         out_specs=(vmem, vmem),
         scratch_shapes=[
-            pltpu.VMEM((flds, levs, wide), jnp.float32),
-            pltpu.VMEM((flds, levs, wide - LANE), jnp.float32),
-            pltpu.VMEM((flds, levs, wide - 2 * LANE), jnp.float32),
-            pltpu.VMEM((tracers, depth, qwide), jnp.float32),
-            pltpu.VMEM((tracers, depth, qwide - LANE), jnp.float32),
-            pltpu.VMEM((nlev, 16, wide), jnp.float32),
-            pltpu.VMEM((24, qwide), jnp.float32),
-            pltpu.VMEM((2, 8, wide), jnp.int32),
-            pltpu.VMEM((2, 8, wide), jnp.float32),
-            pltpu.VMEM((2, 8, qwide), jnp.int32),
-            pltpu.VMEM((2, 8, qwide), jnp.float32),
-            pltpu.VMEM((3, 8, places), jnp.int32),
-            pltpu.VMEM((npos, 8, LANE), jnp.float32),
-            pltpu.VMEM((npos, 8, LANE), jnp.float32),
-            pltpu.VMEM((8, LANE), jnp.float32),
-            dma((2,)),
+            pltpu.SMEM(level_weight.shape, f32),
+            *(pltpu.VMEM(shape, kind) for shape, kind in small),
+            pltpu.VMEM((levs, flds, wide), f32),
+            pltpu.VMEM((rows, wide), f32),
+            pltpu.VMEM((rows, wide - LANE), f32),
+            pltpu.VMEM((rows, wide - 2 * LANE), f32),
+            pltpu.VMEM((2 * wide // LANE - 3, 2 * LANE, 2 * LANE), jnp.bfloat16),
+            pltpu.VMEM((tracers, depth, qwide), f32),
+            pltpu.VMEM((tracers, depth, qwide - LANE), f32),
+            pltpu.VMEM((nlev, 16, wide), f32),
+            pltpu.VMEM((24, qwide), f32),
+            pltpu.VMEM((2, 8, wide), i32),
+            pltpu.VMEM((2, 8, wide), f32),
+            pltpu.VMEM((2, 8, qwide), i32),
+            pltpu.VMEM((2, 8, qwide), f32),
+            pltpu.VMEM((3, 8, places), i32),
+            pltpu.VMEM((npos, 8, LANE), f32),
+            pltpu.VMEM((npos, 8, LANE), f32),
+            dma((11,)),
             dma((3 * nlev,)),
             dma((3 * nlev,)),
-            dma((2,)),
-            dma((2,)),
-            dma((2,)),
-            dma((2,)),
-            dma((2,)),
-            dma((2,)),
-            dma((2,)),
-            dma((2,)),
+            *(dma((2,)) for _ in range(8)),
             dma((npos,)),
             dma((npos,)),
         ],
@@ -428,9 +516,9 @@
             collective_id=0, has_side_effects=True, vmem_limit_bytes=32 * 1024 * 1024
         ),
     )(
-        atmos_state,
+        jnp.transpose(atmos_state, (1, 0, 2)),
         ocean_state,
-        level_weight[:, None],
+        level_weight,
         atmos_neighbors,
         atmos_diffusion,
         ocean_neighbors,
@@ -440,6 +528,28 @@
         read_slots,
         remap_weight,
     )
+    air, sea = pl.pallas_call(
+        move_out,
+        out_shape=(
+            jax.ShapeDtypeStruct((levs, flds, block), f32),
+            jax.ShapeDtypeStruct(ocean_state.shape, f32),
+        ),
+        in_specs=[vmem] * 2,
+        out_specs=(hbm, hbm),
+        scratch_shapes=[dma((2,))],
+    )(air, sea)
+    return jnp.transpose(air, (1, 0, 2)), sea
+
+
+def move_out(air, sea, air_out, sea_out, sems):
+    copies = [
+        pltpu.make_async_copy(air, air_out, sems.at[0]),
+        pltpu.make_async_copy(sea, sea_out, sems.at[1]),
+    ]
+    for copy in copies:
+        copy.start()
+    for copy in copies:
+        copy.wait()
 
 
 def solution(mesh):

time: 25.3 us -> 26.5 us (1.047)
  local copies, waits for them, and re-layouts: 3.54 us -> 8.07 us
  Pallas kernels: 20.8 us -> 17.3 us
    unnamed x22 -> x26, local copies, waits for them, and re-layouts: 2.53 us -> 8.07 us
    pallas_call x1, Pallas kernels: 20.8 us -> 15.5 us  [body(): pl.pallas_call(functools.partial(kernel, npos, nlev), out_shape=(jax.Shap...]
    pallas_call x0 -> x1, Pallas kernels: none -> 1.78 us  [body(): pl.pallas_call(move_out, out_shape=(jax.ShapeDtypeStruct((levs, flds, blo...]
    pallas_call x1 -> x0, local copies, waits for them, and re-layouts: 0.91 us -> none  [body(): pl.pallas_call(functools.partial(kernel, npos, nlev), out_shape=(jax.Shap...]
where the time goes in v2:
time: 26.5 us; the launch traced here: 26.1 us
  Pallas kernels  17.3 us (65%)
  local copies, waits for them, and re-layouts  8.07 us (30%)
  between operations  0.69 us (3%)
    pallas_call x1, Pallas kernels, body(): pl.pallas_call(functools.partial(kernel, npos, nlev), out_shape=(jax.Shap...  15.5 us
    unnamed x26, local copies, waits for them, and re-layouts  8.07 us
    pallas_call x1, Pallas kernels, body(): pl.pallas_call(move_out, out_shape=(jax.ShapeDtypeStruct((levs, flds, blo...  1.78 us

profile of v2, /device:TPU:0, one launch (start us, length us, event | category | flops | bytes accessed | tf_op | source)
XLA Modules:
  0.0 26.1 jit_solution(12718428989322148248)
XLA Ops:
  0.6 0.0 copy-start.8
  0.6 0.0 copy-start.10
  0.7 0.0 copy-start.12
  0.7 0.7 %copy-done.8 = s32[4,256]{1,0:T(4,128)S(1)} copy-done((s32[4,256]{1,0:T(4,128)S(1)}, s32[4,256]{1,0:T(4,128)}, u32[]{:S(2)}) %copy-start.8) | copy-done | bytes 4120
  1.3 0.0 copy-done.10
  1.3 0.0 copy-done.12
  1.3 0.0 copy-start
  1.3 1.0 %copy-done = f32[4,36,512]{2,0,1:T(4,128)S(1)} copy-done((f32[4,36,512]{2,0,1:T(4,128)S(1)}, f32[4,36,512]{2,0,1:T(4,128)}, u32[]{:S(2)}) %copy-start) | copy-done | bytes 294936
  2.3 0.0 copy-start.2
  2.3 0.9 %copy-done.2 = f32[2,80,256]{2,1,0:T(8,128)S(1)} copy-done((f32[2,80,256]{2,1,0:T(8,128)S(1)}, f32[2,80,256]{2,1,0:T(8,128)}, u32[]{:S(2)}) %copy-start.2) | copy-done | bytes 163864
  3.2 0.0 copy-start.4
  3.2 0.7 %copy-done.4 = s32[4,512]{1,0:T(4,128)S(1)} copy-done((s32[4,512]{1,0:T(4,128)S(1)}, s32[4,512]{1,0:T(4,128)}, u32[]{:S(2)}) %copy-start.4) | copy-done | bytes 8216
  3.9 0.0 copy-start.5
  3.9 0.7 %copy-done.5 = f32[4,512]{1,0:T(4,128)S(1)} copy-done((f32[4,512]{1,0:T(4,128)S(1)}, f32[4,512]{1,0:T(4,128)}, u32[]{:S(2)}) %copy-start.5) | copy-done | bytes 8216
  4.6 0.0 copy-start.6
  4.6 0.7 %copy-done.6 = s32[6,256]{1,0:T(8,128)S(1)} copy-done((s32[6,256]{1,0:T(8,128)S(1)}, s32[6,256]{1,0:T(8,128)}, u32[]{:S(2)}) %copy-start.6) | copy-done | bytes 6168
  5.3 0.0 copy-start.7
  5.3 0.7 %copy-done.7 = f32[6,256]{1,0:T(8,128)S(1)} copy-done((f32[6,256]{1,0:T(8,128)S(1)}, f32[6,256]{1,0:T(8,128)}, u32[]{:S(2)}) %copy-start.7) | copy-done | bytes 6168
  6.0 0.0 copy-start.9
  6.0 0.7 %copy-done.9 = f32[4,256]{1,0:T(4,128)S(1)} copy-done((f32[4,256]{1,0:T(4,128)S(1)}, f32[4,256]{1,0:T(4,128)}, u32[]{:S(2)}) %copy-start.9) | copy-done | bytes 4120
  6.7 0.0 copy-start.11
  6.7 0.7 %copy-done.11 = s32[256]{0:T(256)S(1)} copy-done((s32[256]{0:T(256)S(1)}, s32[256]{0:T(256)}, u32[]{:S(2)}) %copy-start.11) | copy-done | bytes 1048
  7.4 15.5 %shard_map.122 = (f32[36,4,512]{2,1,0:T(4,128)S(1)}, f32[2,80,256]{2,1,0:T(8,128)S(1)}) custom-call(f32[36,4,512]{2,1,0:T(4,128)S(1)} %bitcast.4, f32[2,80,256]{2,1,0:T(8,128)S(1)} %copy-done.2, f32[36]{0:T(128)S(1)} %copy-done.12, s32[4,512]{1,0:T(4,128)S(1)} %copy-done.4, f32[4,512]{1,0:T(4,128)S(1)} %copy-done.5, s32[6,256]{1,0:T(8,128)S(1)} %copy-done.6, ...), custom_call_target="tpu_custom_call" | custom-call | tf_op jit(solution)/shard_map/pallas_call | solution.py:481
  22.9 0.0 copy-start.1
  22.9 0.7 %copy-done.1 = f32[36,4,512]{2,1,0:T(4,128)} copy-done((f32[36,4,512]{2,1,0:T(4,128)}, f32[36,4,512]{2,1,0:T(4,128)S(1)}, u32[]{:S(2)}) %copy-start.1) | copy-done | bytes 294936
  23.6 0.0 copy-start.3
  23.6 0.7 %copy-done.3 = f32[2,80,256]{2,1,0:T(8,128)} copy-done((f32[2,80,256]{2,1,0:T(8,128)}, f32[2,80,256]{2,1,0:T(8,128)S(1)}, u32[]{:S(2)}) %copy-start.3) | copy-done | bytes 163864
  24.3 1.8 %shard_map.123 = (f32[36,4,512]{2,1,0:T(4,128)}, f32[2,80,256]{2,1,0:T(8,128)}) custom-call(f32[36,4,512]{2,1,0:T(4,128)} %copy-done.1, f32[2,80,256]{2,1,0:T(8,128)} %copy-done.3), custom_call_target="tpu_custom_call" | custom-call | tf_op jit(solution)/shard_map/pallas_call | solution.py:531
Async XLA Ops:
  0.6 0.7 %copy-start.8 = (s32[4,256]{1,0:T(4,128)S(1)}, s32[4,256]{1,0:T(4,128)}, u32[]{:S(2)}) copy-start(s32[4,256]{1,0:T(4,128)} %rest_6_.1) | copy-start | bytes 12292
  0.6 0.7 %copy-start.10 = (f32[256]{0:T(256)S(1)}, f32[256]{0:T(256)}, u32[]{:S(2)}) copy-start(f32[256]{0:T(256)} %param.18) | copy-start | bytes 3076
  0.7 0.7 %copy-start.12 = (f32[36]{0:T(128)S(1)}, f32[36]{0:T(128)}, u32[]{:S(2)}) copy-start(f32[36]{0:T(128)} %weight_hbm.1) | copy-start | bytes 436
  1.3 1.0 %copy-start = (f32[4,36,512]{2,0,1:T(4,128)S(1)}, f32[4,36,512]{2,0,1:T(4,128)}, u32[]{:S(2)}) copy-start(f32[4,36,512]{2,0,1:T(4,128)} %param.11) | copy-start | bytes 884740
  2.3 0.9 %copy-start.2 = (f32[2,80,256]{2,1,0:T(8,128)S(1)}, f32[2,80,256]{2,1,0:T(8,128)}, u32[]{:S(2)}) copy-start(f32[2,80,256]{2,1,0:T(8,128)} %sea_hbm.1) | copy-start | bytes 491524
  3.2 0.7 %copy-start.4 = (s32[4,512]{1,0:T(4,128)S(1)}, s32[4,512]{1,0:T(4,128)}, u32[]{:S(2)}) copy-start(s32[4,512]{1,0:T(4,128)} %rest_0_.1) | copy-start | bytes 24580
  3.9 0.7 %copy-start.5 = (f32[4,512]{1,0:T(4,128)S(1)}, f32[4,512]{1,0:T(4,128)}, u32[]{:S(2)}) copy-start(f32[4,512]{1,0:T(4,128)} %rest_1_.1) | copy-start | bytes 24580
  4.6 0.7 %copy-start.6 = (s32[6,256]{1,0:T(8,128)S(1)}, s32[6,256]{1,0:T(8,128)}, u32[]{:S(2)}) copy-start(s32[6,256]{1,0:T(8,128)} %rest_2_.1) | copy-start | bytes 18436
  5.3 0.7 %copy-start.7 = (f32[6,256]{1,0:T(8,128)S(1)}, f32[6,256]{1,0:T(8,128)}, u32[]{:S(2)}) copy-start(f32[6,256]{1,0:T(8,128)} %rest_3_.1) | copy-start | bytes 18436
  6.0 0.7 %copy-start.9 = (f32[4,256]{1,0:T(4,128)S(1)}, f32[4,256]{1,0:T(4,128)}, u32[]{:S(2)}) copy-start(f32[4,256]{1,0:T(4,128)} %rest_7_.1) | copy-start | bytes 12292
  6.7 0.7 %copy-start.11 = (s32[256]{0:T(256)S(1)}, s32[256]{0:T(256)}, u32[]{:S(2)}) copy-start(s32[256]{0:T(256)} %param.19) | copy-start | bytes 3076
  22.9 0.7 %copy-start.1 = (f32[36,4,512]{2,1,0:T(4,128)}, f32[36,4,512]{2,1,0:T(4,128)S(1)}, u32[]{:S(2)}) copy-start(f32[36,4,512]{2,1,0:T(4,128)S(1)} %get-tuple-element.6.air) | copy-start | bytes 884740
  23.6 0.7 %copy-start.3 = (f32[2,80,256]{2,1,0:T(8,128)}, f32[2,80,256]{2,1,0:T(8,128)S(1)}, u32[]{:S(2)}) copy-start(f32[2,80,256]{2,1,0:T(8,128)S(1)} %get-tuple-element.7.sea) | copy-start | bytes 491524

commit v3 on v2

--- a/solution.py
+++ b/solution.py
@@ -55,6 +55,8 @@
     send_hbm,
     slot_hbm,
     rw_hbm,
+    air_res,
+    sea_res,
     air_out,
     sea_out,
     weight_ref,
@@ -71,6 +73,7 @@
     xa,
     xb,
     mats,
+    sea_mats,
     y0,
     ya,
     rbuf,
@@ -83,6 +86,8 @@
     pout,
     pin,
     loc_sem,
+    air_sem,
+    out_sem,
     avg_send,
     avg_recv,
     tab_send,
@@ -121,7 +126,16 @@
         for w in (-1, 0, 1):
             pl.semaphore_signal(barrier, inc=1, device_id=at(d + w, l + j), device_id_type=MESH)
 
-    load_air = pltpu.make_async_copy(air_hbm, x0.at[:, :, rim : rim + block], loc_sem.at[0])
+    parts = parts_of(levs)
+    chunk = levs // parts
+    load_air = [
+        pltpu.make_async_copy(
+            air_hbm.at[i * chunk : (i + 1) * chunk],
+            x0.at[i * chunk : (i + 1) * chunk, :, rim : rim + block],
+            air_sem.at[i],
+        )
+        for i in range(parts)
+    ]
     load_sea = pltpu.make_async_copy(sea_hbm, y0.at[:, :, orim : orim + cells], loc_sem.at[1])
     small = [
         pltpu.make_async_copy(src, dst, loc_sem.at[2 + i])
@@ -131,7 +145,8 @@
             (slot_hbm, slot_ref), (rw_hbm, rw_ref),
         ))
     ]
-    load_air.start()
+    for copy in load_air:
+        copy.start()
     for copy in small:
         copy.start()
     load_sea.start()
@@ -155,11 +170,12 @@
     qbuf[21:24, sea_own] = jnp.zeros((3, cells), jnp.float32)
     table[0] = jnp.broadcast_to(send_ref[...], table.shape[1:])
 
-    load_air.wait()
-    sums = [weight_ref[k] * x0[k, :, own] for k in range(4)]
-    for k in range(4, levs):
-        sums[k % 4] = sums[k % 4] + weight_ref[k] * x0[k, :, own]
-    rbuf[0, 0:flds, own] = (sums[0] + sums[1]) + (sums[2] + sums[3])
+    mean = jnp.zeros((flds, block), jnp.float32)
+    for i in range(parts):
+        load_air[i].wait()
+        for k in range(i * chunk, (i + 1) * chunk):
+            mean = mean + weight_ref[k] * x0[k, :, own]
+    rbuf[0, 0:flds, own] = mean
     load_sea.wait()
 
     pl.semaphore_wait(barrier, npos - 1 + 3 * (nlev - 1))
@@ -219,13 +235,30 @@
     row_ids = lax.broadcasted_iota(jnp.int32, (2 * LANE, LANE), 0)
     self_ids = lane_of((2 * LANE, LANE)) + HALO
 
-    def build(index, places, rates, keep):
+    def build(index, places, rates, keep, out=mats):
         matrix = jnp.where(row_ids == self_ids, keep, 0.0)
-        for n in range(nba):
+        for n in range(places.shape[0]):
             matrix = matrix + jnp.where(row_ids == places[n : n + 1], rates[n : n + 1], 0.0)
         upper = matrix.astype(jnp.bfloat16)
-        mats[index, :, 0:LANE] = upper
-        mats[index, :, LANE:] = (matrix - upper.astype(jnp.float32)).astype(jnp.bfloat16)
+        out[index, :, 0:LANE] = upper
+        out[index, :, LANE:] = (matrix - upper.astype(jnp.float32)).astype(jnp.bfloat16)
+
+    def apply(x, matrix):
+        count = x.shape[0]
+        upper = x.astype(jnp.bfloat16)
+        lower = (x - upper.astype(jnp.float32)).astype(jnp.bfloat16)
+        both = jnp.concatenate([upper, lower], axis=0)
+        prod = jnp.dot(both, matrix, preferred_element_type=jnp.float32)
+        rest_sum = prod[count:, 0:LANE] + prod[:count, LANE:] + prod[count:, LANE:]
+        return prod[:count, 0:LANE] + rest_sum
+
+    def sea_tables(data, shift):
+        span = data.shape[1]
+        moved = pltpu.roll(data, span - HALO, axis=1) if shift else data
+        rates = moved[6 : 6 + nbo]
+        tile_lane = jnp.bitwise_and(lane_of((nbo, span)), LANE - 1)
+        places = moved[0:nbo].astype(jnp.int32) + tile_lane + HALO
+        return places, rates, 1.0 - jnp.sum(rates, axis=0, keepdims=True), moved[12:13]
 
     wide = rbuf.shape[2]
     own_data = rbuf[0, :, own]
@@ -245,6 +278,16 @@
             xf[4 * k : 4 * k + 8, cols] = jnp.concatenate([x0[k, :, cols], x0[k + 1, :, cols]], axis=0)
 
     flatten(own)
+
+    sea_shifted = qbuf.shape[1] // LANE - 1
+    sea_done = set()
+    for shift in range(2):
+        places, rates, keep, _ = sea_tables(qbuf[:, sea_own], shift)
+        for t in range(cells // LANE - shift):
+            cols = slice(t * LANE, (t + 1) * LANE)
+            index = orim // LANE + t + (0 if shift else sea_shifted - 1)
+            build(index, places[:, cols], rates[:, cols], keep[:, cols], sea_mats)
+            sea_done.add(index)
 
     for copy in avg:
         copy.wait_recv()
@@ -315,13 +358,17 @@
     qall = qbuf[...]
     qwide = qall.shape[1]
     for shift in range(2):
-        moved = pltpu.roll(qall, qwide - HALO, axis=1) if shift else qall
-        rates = moved[6 : 6 + nbo]
-        tile_lane = jnp.bitwise_and(lane_of((nbo, qwide)), LANE - 1)
-        oplace[shift, 0:nbo] = moved[0:nbo].astype(jnp.int32) + tile_lane + HALO
+        places, rates, keep, mixing = sea_tables(qall, shift)
+        oplace[shift, 0:nbo] = places
         orate[shift, 0:nbo] = rates
-        orate[shift, nbo : nbo + 1] = 1.0 - jnp.sum(rates, axis=0, keepdims=True)
-        orate[shift, nbo + 1 : nbo + 2] = moved[12:13]
+        orate[shift, nbo : nbo + 1] = keep
+        orate[shift, nbo + 1 : nbo + 2] = mixing
+        for t in range(1 - shift, sea_shifted):
+            index = t + (0 if shift else sea_shifted - 1)
+            if index in sea_done or (shift == 0 and t > cells // LANE):
+                continue
+            cols = slice(t * LANE, (t + 1) * LANE)
+            build(index, places[:, cols], rates[:, cols], keep[:, cols], sea_mats)
 
     def sea_cols(k, t):
         base = (k + 1) // 2
@@ -339,23 +386,21 @@
         return orate[shift, nbo + 1 : nbo + 2, cols]
 
     src = y0
+    tracers, depth = y0.shape[0], y0.shape[1]
+    level = lax.broadcasted_iota(jnp.int32, (depth, LANE), 0)
     for k in range(STEPS_OCN):
         dst = sea_out if k == STEPS_OCN - 1 else ya
-
-        def sea_step(tracer, carry, k=k, src=src, dst=dst):
-            depth = src.shape[1]
-            level = lax.broadcasted_iota(jnp.int32, (depth, LANE), 0)
-            for t in range(dst.shape[2] // LANE):
-                first = src[tracer, :, t * LANE : (t + 1) * LANE]
-                second = src[tracer, :, (t + 1) * LANE : (t + 2) * LANE]
-                v = sea_tile(k, t, first, second)
+        for t in range(dst.shape[2] // LANE):
+            shift, base = 1 - k % 2, (k + 1) // 2
+            index = base + t + (0 if shift else sea_shifted - 1)
+            x = src[:, :, t * LANE : (t + 2) * LANE].reshape(tracers * depth, 2 * LANE)
+            mixed = apply(x, sea_mats[index])
+            for tracer in range(tracers):
+                v = mixed[tracer * depth : (tracer + 1) * depth]
                 up = jnp.where(level == 0, v, pltpu.roll(v, 1, axis=0))
                 down = jnp.where(level == depth - 1, v, pltpu.roll(v, depth - 1, axis=0))
                 v = v + sea_vertical(k, t) * (up - 2.0 * v + down)
                 dst[tracer, :, t * LANE : (t + 1) * LANE] = v
-            return carry
-
-        lax.fori_loop(0, src.shape[0], sea_step, 0)
         src = dst
 
     for shift in range(2):
@@ -372,7 +417,6 @@
         copy.wait_recv()
     flatten(lefts)
     flatten(rights)
-    rows = xf.shape[0]
     src = xf
     for k in range(STEPS_ATM):
         dst = xa if k % 2 == 0 else xb
@@ -380,12 +424,7 @@
             shift, base = 1 - k % 2, (k + 1) // 2
             index = base + t + (0 if shift else shifted_count - 1)
             x = src[:, t * LANE : (t + 2) * LANE]
-            upper = x.astype(jnp.bfloat16)
-            lower = (x - upper.astype(jnp.float32)).astype(jnp.bfloat16)
-            both = jnp.concatenate([upper, lower], axis=0)
-            prod = jnp.dot(both, mats[index], preferred_element_type=jnp.float32)
-            small_part = prod[rows:, 0:LANE] + prod[:rows, LANE:] + prod[rows:, LANE:]
-            result = prod[:rows, 0:LANE] + small_part
+            result = apply(x, mats[index])
             cols = slice(t * LANE, (t + 1) * LANE)
             if k < STEPS_ATM - 1:
                 dst[:, cols] = result
@@ -393,36 +432,52 @@
                 for level in range(levs):
                     air_out[level, :, cols] = result[4 * level : 4 * level + 4]
         src = dst
-
-    for copy in routes:
-        copy.wait_recv()
+    save_air = [
+        pltpu.make_async_copy(
+            air_out.at[i * chunk : (i + 1) * chunk],
+            air_res.at[i * chunk : (i + 1) * chunk],
+            out_sem.at[i],
+        )
+        for i in range(parts)
+    ]
+    for copy in save_air:
+        copy.start()
+
     sub8 = lax.broadcasted_iota(jnp.int32, (8, LANE), 0)
     kinds = [jnp.where(s == 0, 2, 0)] + [s] * (cells // LANE) + [jnp.where(s == 0, 1, 2)]
-    changes = []
+    bits = cap.bit_length() - 1
+    ready = []
     for t in range(qwide // LANE):
         cols = slice(t * LANE, (t + 1) * LANE)
         slots = qbuf[13 : 13 + krem, cols].astype(jnp.int32)
         weights = qbuf[17 : 17 + krem, cols]
-        acc = jnp.zeros((8, LANE), jnp.float32)
+        weights = weights / jnp.sum(weights, axis=0, keepdims=True)
+        terms = []
         for m in range(krem // 2):
             m2 = m + krem // 2
             slot = jnp.where(sub8 < 4, slots[m : m + 1], slots[m2 : m2 + 1])
             weight2 = jnp.where(sub8 < 4, weights[m : m + 1], weights[m2 : m2 + 1])
-            far = lax.rem(d - slot // cap + npos, npos)
-            lanes = lax.rem(slot, cap) + kinds[t] * cap
+            far = d - lax.shift_right_logical(slot, bits)
+            far = jnp.where(far < 0, far + npos, far)
+            terms.append((far, jnp.bitwise_and(slot, cap - 1) + kinds[t] * cap, weight2))
+        sst = y0[0, 0:1, cols]
+        ready.append((terms, sst, 0.5 * jnp.exp(0.25 * sst), 1.0 + 0.2 * y0[1, 0:1, cols]))
+    for copy in routes:
+        copy.wait_recv()
+    changes = []
+    for terms, sst, humid_sea, brine_rate in ready:
+        acc = jnp.zeros((8, LANE), jnp.float32)
+        for far, lanes, weight2 in terms:
             value = pick(pin[0], lanes)
             for k in range(1, npos):
                 value = jnp.where(far == k, pick(pin[k], lanes), value)
             acc = acc + weight2 * value
         acc = acc + pltpu.roll(acc, 4, axis=0)
-        acc = acc / jnp.sum(weights, axis=0, keepdims=True)
         temp, humid, east, north = (acc[i : i + 1] for i in range(4))
-        sst = y0[0, 0:1, cols]
-        salt = y0[1, 0:1, cols]
         wind = jnp.sqrt(east * east + north * north + 1.0)
-        evap = 0.2 * wind * (0.5 * jnp.exp(0.25 * sst) - humid)
+        evap = 0.2 * wind * (humid_sea - humid)
         heat = 0.3 * wind * (temp - sst) - 1.5 * evap
-        brine = 0.5 * evap * (1.0 + 0.2 * salt)
+        brine = 0.5 * evap * brine_rate
         changes.append(jnp.where(sub8 == 0, heat, jnp.where(sub8 == 1, brine, 0.0)))
     later = []
     for t in range(len(changes) - 1):
@@ -439,8 +494,12 @@
             sea_out[tracer, 1:2, cols] += b + mixing * (a - 2.0 * b)
             sea_out[tracer, 2:3, cols] += mixing * b
 
+    save_sea = pltpu.make_async_copy(sea_out, sea_res, loc_sem.at[0])
+    save_sea.start()
     for copy in avg + tabs + qs + seas + airs + routes:
         copy.wait_send()
+    for copy in save_air + [save_sea]:
+        copy.wait()
 
 
 def body(
@@ -485,8 +544,10 @@
             jax.ShapeDtypeStruct(ocean_state.shape, f32),
         ),
         in_specs=[hbm] * 11,
-        out_specs=(vmem, vmem),
+        out_specs=(hbm, hbm),
         scratch_shapes=[
+            pltpu.VMEM((levs, flds, block), f32),
+            pltpu.VMEM(ocean_state.shape, f32),
             pltpu.SMEM(level_weight.shape, f32),
             *(pltpu.VMEM(shape, kind) for shape, kind in small),
             pltpu.VMEM((levs, flds, wide), f32),
@@ -494,6 +555,7 @@
             pltpu.VMEM((rows, wide - LANE), f32),
             pltpu.VMEM((rows, wide - 2 * LANE), f32),
             pltpu.VMEM((2 * wide // LANE - 3, 2 * LANE, 2 * LANE), jnp.bfloat16),
+            pltpu.VMEM((2 * qwide // LANE - 3, 2 * LANE, 2 * LANE), jnp.bfloat16),
             pltpu.VMEM((tracers, depth, qwide), f32),
             pltpu.VMEM((tracers, depth, qwide - LANE), f32),
             pltpu.VMEM((nlev, 16, wide), f32),
@@ -506,6 +568,8 @@
             pltpu.VMEM((npos, 8, LANE), f32),
             pltpu.VMEM((npos, 8, LANE), f32),
             dma((11,)),
+            dma((parts_of(levs),)),
+            dma((parts_of(levs),)),
             dma((3 * nlev,)),
             dma((3 * nlev,)),
             *(dma((2,)) for _ in range(8)),
@@ -513,7 +577,7 @@
             dma((npos,)),
         ],
         compiler_params=pltpu.CompilerParams(
-            collective_id=0, has_side_effects=True, vmem_limit_bytes=32 * 1024 * 1024
+            collective_id=0, has_side_effects=True, vmem_limit_bytes=60 * 1024 * 1024
         ),
     )(
         jnp.transpose(atmos_state, (1, 0, 2)),
@@ -536,16 +600,27 @@
         ),
         in_specs=[vmem] * 2,
         out_specs=(hbm, hbm),
-        scratch_shapes=[dma((2,))],
+        scratch_shapes=[dma((parts_of(levs),)), dma((2,))],
     )(air, sea)
     return jnp.transpose(air, (1, 0, 2)), sea
 
 
-def move_out(air, sea, air_out, sea_out, sems):
+def parts_of(levs):
+    return next(n for n in (6, 4, 3, 2, 1) if levs % n == 0)
+
+
+def move_out(air, sea, air_out, sea_out, sems, sea_sems):
+    parts = parts_of(air.shape[0])
+    chunk = air.shape[0] // parts
     copies = [
-        pltpu.make_async_copy(air, air_out, sems.at[0]),
-        pltpu.make_async_copy(sea, sea_out, sems.at[1]),
+        pltpu.make_async_copy(
+            air.at[i * chunk : (i + 1) * chunk],
+            air_out.at[i * chunk : (i + 1) * chunk],
+            sems.at[i],
+        )
+        for i in range(parts)
     ]
+    copies += [pltpu.make_async_copy(sea.at[i], sea_out.at[i], sea_sems.at[i]) for i in range(2)]
     for copy in copies:
         copy.start()
     for copy in copies:

time: 26.5 us -> 18.1 us (0.68)
  local copies, waits for them, and re-layouts: 8.07 us -> 0 us
    unnamed x26 -> x0, local copies, waits for them, and re-layouts: 8.07 us -> none
where the time goes in v3:
time: 18.1 us; the launch traced here: 17.9 us
  Pallas kernels  17.3 us (96%)
  between operations  0.64 us (4%)
    pallas_call x1, Pallas kernels, body(): pl.pallas_call(functools.partial(kernel, npos, nlev), out_shape=(jax.Shap...  15.4 us
    pallas_call x1, Pallas kernels, body(): pl.pallas_call(move_out, out_shape=(jax.ShapeDtypeStruct((levs, flds, blo...  1.83 us

profile of v3, /device:TPU:0, one launch (start us, length us, event | category | flops | bytes accessed | tf_op | source)
XLA Modules:
  0.0 17.9 jit_solution(157020455506494195)
XLA Ops:
  0.6 15.4 %shard_map.122 = (f32[36,4,512]{2,1,0:T(4,128)}, f32[2,80,256]{2,1,0:T(8,128)}) custom-call(f32[36,4,512]{2,1,0:T(4,128)} %bitcast.4, f32[2,80,256]{2,1,0:T(8,128)} %sea_hbm.1, f32[36]{0:T(128)} %weight_hbm.1, s32[4,512]{1,0:T(4,128)} %rest_0_.1, f32[4,512]{1,0:T(4,128)} %rest_1_.1, s32[6,256]{1,0:T(8,128)} %rest_2_.1, f32[6,256]{1,0:T(8,128)} %rest_3_.1, ...), custom_call_target="tpu_custom_call" | custom-call | tf_op jit(solution)/shard_map/pallas_call | solution.py:540
  16.1 1.8 %shard_map.123 = (f32[36,4,512]{2,1,0:T(4,128)}, f32[2,80,256]{2,1,0:T(8,128)}) custom-call(f32[36,4,512]{2,1,0:T(4,128)} %get-tuple-element.6.air, f32[2,80,256]{2,1,0:T(8,128)} %get-tuple-element.7.sea), custom_call_target="tpu_custom_call" | custom-call | tf_op jit(solution)/shard_map/pallas_call | solution.py:595
